TPU v7x, 32 devices: a whole 2x2x4 slice. The times are simulated.
32 devices in a mesh: dp: 8 (over z, y), cent: 4 (over x, core).
Axes of the slice: x: 2, y: 2, z: 4, core: 2. Of those that a mesh axis runs over, the one named last changes fastest.
Arguments:
- embeddings: bfloat16 [6144, 768], P('dp'), may hold values from -40 to 40
- centroids: bfloat16 [16384, 768], P('cent'), may hold values from -5 to 5
- rotation: float32 [768, 768], replicated, may hold values from -1 to 2
Outputs:
- new_centroids: float32 [16384, 768], P(('cent', 'dp'))
- new_rotation: float32 [768, 768], replicated
All inputs are finite; a program needn't handle non-finite values.
Results may differ from a plain program's by a relative error of at most 0.0042.
Values sent between devices are 32-bit elements; how exact they have to be, the bound alone decides.
A program may use at most 128 MiB of HBM per device.

v0:
```python
import math

import jax
import jax.numpy as jnp
from jax import lax
from jax.sharding import PartitionSpec as P

NS_ITERS = 4


SHARPNESS = 3.0
PRIOR_WEIGHT = 0.25
EPSILON = 1e-06


def body(embeddings, centroids, rotation):
    highest = lax.Precision.HIGHEST
    width = rotation.shape[0]
    rows_wide = embeddings.astype(jnp.float32)
    rotated = jnp.dot(rows_wide, rotation, precision=highest).astype(jnp.bfloat16)
    half_norm = 0.5 * jnp.sum(jnp.square(centroids.astype(jnp.float32)), axis=1)
    score_scale = SHARPNESS / math.sqrt(width)
    raw_scores = lax.dot_general(
        rotated, centroids, (((1,), (1,)), ((), ())), preferred_element_type=jnp.float32
    )
    scores = (raw_scores - half_norm[None, :]) * score_scale
    row_top = lax.pmax(jnp.max(scores, axis=1), "cent")
    exp_scores = jnp.exp(scores - row_top[:, None])
    row_total = lax.psum(jnp.sum(exp_scores, axis=1), "cent")
    weights = (exp_scores / row_total[:, None]).astype(jnp.bfloat16)
    cent_sums = lax.dot_general(
        weights, rotated, (((0,), (0,)), ((), ())), preferred_element_type=jnp.float32
    )
    counts = jnp.sum(weights.astype(jnp.float32), axis=0)
    share_sums, share_counts = (
        lax.psum_scatter(cent_sums, "dp", scatter_dimension=0, tiled=True),
        lax.psum_scatter(counts, "dp", scatter_dimension=0, tiled=True),
    )
    block_rows = share_sums.shape[0]
    first_row = lax.axis_index("dp") * block_rows
    own_centroids = lax.dynamic_slice_in_dim(centroids, first_row, block_rows, 0).astype(
        jnp.float32
    )
    new_centroids = (share_sums + PRIOR_WEIGHT * own_centroids) / (share_counts + PRIOR_WEIGHT)[
        :, None
    ]
    rebuilt = jnp.dot(weights, centroids, preferred_element_type=jnp.float32)
    partial_value = jnp.dot(rows_wide.T, rebuilt, precision=highest)
    cross_gram = lax.psum(partial_value, ("dp", "cent"))
    frobenius = jnp.sqrt(jnp.sum(cross_gram * cross_gram) + EPSILON)
    unit_cross = cross_gram / frobenius
    gram_once = jnp.dot(unit_cross.T, unit_cross, precision=highest)
    gram_twice = jnp.dot(gram_once, gram_once, precision=highest)
    norm_scale = (jnp.sum(gram_twice * gram_twice) + EPSILON) ** 0.125
    iterate = unit_cross / norm_scale
    for iteration in range(NS_ITERS):
        inner = jnp.dot(iterate.T, iterate, precision=highest)
        iterate = 1.5 * iterate - 0.5 * jnp.dot(iterate, inner, precision=highest)
    return (new_centroids, iterate)


def solution(mesh):
    in_specs = (P("dp", None), P("cent", None), P())
    out_specs = (P(("cent", "dp"), None), P())
    return jax.shard_map(body, mesh=mesh, in_specs=in_specs, out_specs=out_specs, check_vma=False)
```

profile of v0, /device:TPU:0, one launch (start us, length us, event | category | flops | bytes accessed | tf_op | source)
XLA Modules:
  0.0 409.0 jit_solution(15774380392176868603)
XLA Ops:
  8.0 0.0 all-reduce.3.cloned.1.call-start
  8.1 4.2 %multiply_reduce_fusion = f32[4096]{0:T(1024)S(1)} fusion(bf16[4096,768]{1,0:T(8,128)(2,1)} %param.4), kind=kLoop, calls=%fused_computation.4 | loop fusion | flops 9433088 | bytes 6307840 | tf_op jit(solution)/shard_map/reduce_sum | solution.py:21
  12.4 3.0 convolution_convert_fusion
  15.4 8.1 %fusion = (f32[768]{0:T(1024)S(1)}, f32[768,4096]{1,0:T(8,128)}) fusion(f32[4096]{0:T(1024)S(1)} %broadcast_multiply_fusion, bf16[768,768]{1,0:T(8,128)(2,1)S(1)} %convolution_convert_fusion, bf16[4096,768]{1,0:T(8,128)(2,1)S(1)} %copy-done.2), kind=kOutput, calls=%fused_computation.5 | convolution fusion | flops 4841274368 | bytes 20073472 | tf_op jit(solution)/shard_map/dot_general | solution.py:23
  23.5 8.3 %pmax.7 = f32[768]{0:T(1024)S(1)} all-reduce(f32[768]{0:T(1024)S(1)} %get-tuple-element.8), channel_id=1, replica_groups=mesh['dp'=8,'cent'=4] {'cent'}, use_global_device_ids=true, to_apply=%region_2.0 | all-reduce | flops 768 | bytes 6144 | tf_op jit(solution)/shard_map/pmax | solution.py:27
  31.9 6.4 %fusion.1 = f32[768]{0:T(1024)S(1)} fusion(f32[768,4096]{1,0:T(8,128)} %get-tuple-element.9, f32[768]{0:T(1024)S(1)} %pmax.7, f32[4096]{0:T(1024)S(1)} %broadcast_multiply_fusion), kind=kLoop, calls=%fused_computation.6 | loop fusion | flops 12582144 | bytes 12605440 | tf_op jit(solution)/shard_map/reduce_sum | solution.py:29
  38.2 5.9 %psum.14 = f32[768]{0:T(1024)S(1)} all-reduce(f32[768]{0:T(1024)S(1)} %fusion.1), channel_id=1, replica_groups=mesh['dp'=8,'cent'=4] {'cent'}, use_global_device_ids=true, to_apply=%region_4.0 | all-reduce | flops 768 | bytes 6144 | tf_op jit(solution)/shard_map/psum | solution.py:29
  44.2 6.8 %convert_reduce_fusion = (f32[4096]{0:T(1024)S(1)}, bf16[768,4096]{1,0:T(8,128)(2,1)S(1)}) fusion(f32[768]{0:T(1024)S(1)} %psum.14, f32[768]{0:T(1024)S(1)} %pmax.7, f32[768,4096]{1,0:T(8,128)} %get-tuple-element.9, f32[4096]{0:T(1024)S(1)} %broadcast_multiply_fusion), kind=kLoop, calls=%fused_computation | loop fusion | flops 22016000 | bytes 18913280 | tf_op jit(solution)/shard_map/reduce_sum | solution.py:34
  51.0 8.8 %fusion.7 = f32[768,768]{1,0:T(8,128)S(1)} fusion(bf16[768,4096]{1,0:T(8,128)(2,1)S(1)} %get-tuple-element.7, bf16[4096,768]{1,0:T(8,128)(2,1)} %param.4), kind=kOutput, calls=%fused_computation.24 | convolution fusion | flops 4831838208 | bytes 14942208 | tf_op jit(solution)/shard_map/dot_general | solution.py:47
  59.9 4.7 %convolution_bitcast_fusion = f32[768,768]{0,1:T(8,128)} fusion(f32[768,768]{1,0:T(8,128)S(1)} %fusion.7, bf16[768,768]{1,0:T(8,128)(2,1)S(1)} %copy-done.5), kind=kOutput, calls=%fused_computation.15 | convolution fusion | flops 5435817984 | bytes 5898240 | tf_op jit(solution)/shard_map/dot_general | solution.py:48
  64.6 0.0 reduce-scatter.2.cloned.1.call-start
  64.6 1.2 copy-done.8
  65.8 10.6 %fusion.6 = f32[4096,768]{1,0:T(8,128)} fusion(bf16[768,4096]{1,0:T(8,128)(2,1)} %copy-done.3, bf16[768,768]{1,0:T(8,128)(2,1)S(1)} %copy-done.8), kind=kOutput, calls=%fused_computation.23 | convolution fusion | flops 4831838208 | bytes 20054016 | tf_op jit(solution)/shard_map/dot_general | solution.py:31
  76.4 0.0 reduce-scatter.2.cloned.1.call-update
  76.5 0.6 copy-done.6
  77.1 0.6 dynamic-slice
  78.3 39.7 %all-reduce = f32[4096]{0:T(1024)S(1)} all-reduce(f32[4096]{0:T(1024)S(1)} %get-tuple-element.6), channel_id=3, replica_groups=mesh['dp'=8,'cent'=4] {'dp'}, use_global_device_ids=true, to_apply=%region_7.0.clone | all-reduce | flops 4096 | bytes 32768
  118.0 0.1 dynamic-slice_add_fusion
  118.1 207.2 %all-reduce.3.cloned.1.call-done = f32[768,768]{0,1:T(8,128)} async-done(((f32[768,768]{0,1:T(8,128)}), f32[768,768]{0,1:T(8,128)}) %all-reduce.3.cloned.1.call-update) | async-done | bytes 2359312 | tf_op jit(solution)/shard_map/psum | solution.py:49
  325.3 3.0 multiply_reduce_fusion.2
  329.0 6.0 %fusion.2 = f32[768,768]{1,0:T(8,128)S(1)} fusion(f32[768,768]{0,1:T(8,128)S(1)} %copy-done.4, f32[]{:T(128)S(6)} %sqrt.3), kind=kOutput, calls=%fused_computation.12 | convolution fusion | flops 5436407808 | bytes 4718596 | tf_op jit(solution)/shard_map/dot_general | solution.py:52
  335.1 6.4 %multiply_reduce_fusion.1 = f32[]{:T(128)} fusion(f32[768,768]{1,0:T(8,128)S(1)} %fusion.2), kind=kOutput, calls=%fused_computation.11 | convolution fusion | flops 5436997632 | bytes 2359300 | tf_op jit(solution)/shard_map/dot_general | solution.py:53
  342.2 6.4 %fusion.5 = f32[768,768]{1,0:T(8,128)S(1)} fusion(f32[768,768]{0,1:T(8,128)S(1)} %copy-done.4, f32[]{:T(128)S(6)} %multiply.4), kind=kOutput, calls=%fused_computation.20 | convolution fusion | flops 5436407808 | bytes 4718596 | tf_op jit(solution)/shard_map/dot_general | solution.py:57
  348.6 6.8 %multiply_subtract_fusion.3 = f32[768,768]{0,1:T(8,128)S(1)} fusion(f32[768,768]{1,0:T(8,128)S(1)} %fusion.5, f32[768,768]{0,1:T(8,128)S(1)} %copy-done.4, f32[]{:T(128)S(6)} %multiply.4), kind=kOutput, calls=%fused_computation.10 | convolution fusion | flops 5438767104 | bytes 7077892 | tf_op jit(solution)/shard_map/dot_general | solution.py:58
  355.4 6.1 %fusion.8 = f32[768,768]{1,0:T(8,128)S(1)} fusion(f32[768,768]{0,1:T(8,128)S(1)} %multiply_subtract_fusion.3), kind=kOutput, calls=%fused_computation.25 | convolution fusion | flops 5435817984 | bytes 4718592 | tf_op jit(solution)/shard_map/dot_general | solution.py:57
  361.6 6.6 %multiply_subtract_fusion.2 = f32[768,768]{0,1:T(8,128)S(1)} fusion(f32[768,768]{0,1:T(8,128)S(1)} %multiply_subtract_fusion.3, f32[768,768]{1,0:T(8,128)S(1)} %fusion.8), kind=kOutput, calls=%fused_computation.9 | convolution fusion | flops 5437587456 | bytes 7077888 | tf_op jit(solution)/shard_map/dot_general | solution.py:58
  368.2 6.4 %fusion.9 = f32[768,768]{1,0:T(8,128)S(1)} fusion(f32[768,768]{0,1:T(8,128)S(1)} %multiply_subtract_fusion.2), kind=kOutput, calls=%fused_computation.26 | convolution fusion | flops 5435817984 | bytes 4718592 | tf_op jit(solution)/shard_map/dot_general | solution.py:57
  374.6 6.8 %multiply_subtract_fusion.1 = f32[768,768]{0,1:T(8,128)S(1)} fusion(f32[768,768]{0,1:T(8,128)S(1)} %multiply_subtract_fusion.2, f32[768,768]{1,0:T(8,128)S(1)} %fusion.9), kind=kOutput, calls=%fused_computation.8 | convolution fusion | flops 5437587456 | bytes 7077888 | tf_op jit(solution)/shard_map/dot_general | solution.py:58
  381.4 6.0 %fusion.10 = f32[768,768]{1,0:T(8,128)S(1)} fusion(f32[768,768]{0,1:T(8,128)S(1)} %multiply_subtract_fusion.1), kind=kOutput, calls=%fused_computation.27 | convolution fusion | flops 5435817984 | bytes 4718592 | tf_op jit(solution)/shard_map/dot_general | solution.py:57
  387.4 7.7 %multiply_subtract_fusion = f32[768,768]{0,1:T(8,128)} fusion(f32[768,768]{0,1:T(8,128)S(1)} %multiply_subtract_fusion.1, f32[768,768]{1,0:T(8,128)S(1)} %fusion.10), kind=kOutput, calls=%fused_computation.7 | convolution fusion | flops 5437587456 | bytes 7077888 | tf_op jit(solution)/shard_map/dot_general | solution.py:58
  395.2 3.2 copy.14
  398.4 3.0 add_divide_fusion
  (19 shorter events, 0.1 us)
Async XLA Ops:
  8.0 4.3 %copy-start = (f32[768,768]{1,0:T(8,128)S(1)}, f32[768,768]{1,0:T(8,128)}, u32[]{:S(2)}) copy-start(f32[768,768]{1,0:T(8,128)} %param.5) | copy-start | bytes 7077892
  8.0 4.3 %copy-start.5 = (bf16[768,768]{1,0:T(8,128)(2,1)S(1)}, bf16[768,768]{1,0:T(8,128)(2,1)}, u32[]{:S(2)}) copy-start(bf16[768,768]{1,0:T(8,128)(2,1)} %param.3) | copy-start | bytes 3538948
  8.0 317.3 %all-reduce.3.cloned.1.call-start = ((), (), s32[]{:S(2)}) async-start(), calls=%async_computation.2 | async-start | bytes 4718592 | tf_op jit(solution)/shard_map/psum | solution.py:49
  8.1 7.3 %copy-start.2 = (bf16[4096,768]{1,0:T(8,128)(2,1)S(1)}, bf16[4096,768]{1,0:T(8,128)(2,1)}, u32[]{:S(2)}) copy-start(bf16[4096,768]{1,0:T(8,128)(2,1)} %param.4) | copy-start | bytes 18874372
  15.4 8.1 %copy-start.7 = (bf16[768,768]{1,0:T(8,128)(2,1)}, bf16[768,768]{1,0:T(8,128)(2,1)S(1)}, u32[]{:S(2)}) copy-start(bf16[768,768]{1,0:T(8,128)(2,1)S(1)} %convolution_convert_fusion) | copy-start | bytes 3538948
  51.0 8.9 %copy-start.3 = (bf16[768,4096]{1,0:T(8,128)(2,1)}, bf16[768,4096]{1,0:T(8,128)(2,1)S(1)}, u32[]{:S(2)}) copy-start(bf16[768,4096]{1,0:T(8,128)(2,1)S(1)} %get-tuple-element.7) | copy-start | bytes 18874372
  64.5 1.3 copy-start.8
  64.6 333.8 %reduce-scatter.2.cloned.1.call-start = ((), (), s32[]{:S(2)}) async-start(), calls=%async_computation.1 | async-start | bytes 14155776 | tf_op jit(solution)/shard_map/reduce_scatter | solution.py:36
  76.4 0.7 copy-start.6
  325.3 3.7 copy-start.4
  395.2 6.2 %copy-start.1 = (f32[768,768]{1,0:T(8,128)S(1)}, f32[768,768]{1,0:T(8,128)}, u32[]{:S(2)}) copy-start(f32[768,768]{1,0:T(8,128)} %param.5) | copy-start | bytes 7077892
Sparse Core Ops, SparseCore 0:
  64.7 260.5 all-reduce.2
Sparse Core Ops, SparseCore 1:
  76.6 213.4 reduce-scatter.1
where the time goes:
time: 415 us; the launch traced here: 409 us
  waiting for transfers between devices  207 us (50%)
  matrix products  101 us (24%)
  blocking collectives  53.9 us (13%)
  other arithmetic  23.5 us (6%)
  between operations  17.9 us (4%)
  local copies, waits for them, and re-layouts  5.63 us (1%)
    psum x1, waiting for transfers between devices, body(): cross_gram = lax.psum(partial_value, ('dp', 'cent'))  207 us
    unnamed x1, blocking collectives  39.7 us
    dot_general x4, matrix products, body(): iterate = 1.5 * iterate - 0.5 * jnp.dot(iterate, inner, precision=highest)  28 us
    dot_general x4, matrix products, body(): inner = jnp.dot(iterate.T, iterate, precision=highest)  25 us
    dot_general x1, matrix products, body(): lax.dot_general(weights, rotated, (((0,), (0,)), ((), ())), preferred_ele...  10.6 us
    dot_general x1, matrix products, body(): rebuilt = jnp.dot(weights, centroids, preferred_element_type=jnp.float32)  8.84 us
    pmax x1, blocking collectives, body(): row_top = lax.pmax(jnp.max(scores, axis=1), 'cent')  8.31 us
  transfers between devices with their start and end apart: 2, of which 1 were waited for; matrix products, arithmetic and copies ran while one was open for 20% of the time, Pallas kernels for 0%

commit v1 on v0

v1 whole, which is shorter than its diff:
```python
import functools
import math

import jax
import jax.numpy as jnp
from jax import lax
from jax.experimental import pallas as pl
from jax.experimental.pallas import tpu as pltpu
from jax.sharding import PartitionSpec as P

NS_ITERS = 4
SHARPNESS = 3.0
PRIOR_WEIGHT = 0.25
EPSILON = 1e-06
GROUP = 4
TILE = 512
VMEM_BYTES = 56 * 1024 * 1024

f32, bf16 = jnp.float32, jnp.bfloat16


def dot(a, b, ca, cb):
    return lax.dot_general(a, b, (((ca,), (cb,)), ((), ())), preferred_element_type=f32)


def half_norms(block):
    wide = block.astype(f32)
    return 0.5 * jnp.sum(wide * wide, axis=1, keepdims=True)


def stats_kernel(scale, rot_ref, cent_ref, exp_ref, tile_top_ref, stat_ref, rot_s, run_s):
    step = pl.program_id(0)

    @pl.when(step == 0)
    def _():
        rot_s[...] = rot_ref[...].astype(bf16)
        run_s[0:1, :] = jnp.full((1, run_s.shape[1]), -jnp.inf, f32)
        run_s[1:2, :] = jnp.zeros((1, run_s.shape[1]), f32)

    cents = cent_ref[...]
    scores = (dot(cents, rot_s[...], 1, 1) - half_norms(cents)) * scale
    old_top = run_s[0:1, :]
    top = jnp.maximum(old_top, jnp.max(scores, axis=0, keepdims=True))
    exps = jnp.exp(scores - top)
    total = run_s[1:2, :] * jnp.exp(old_top - top) + jnp.sum(exps, axis=0, keepdims=True)
    exp_ref[...] = exps
    tile_top_ref[0] = top
    run_s[0:1, :] = top
    run_s[1:2, :] = total
    stat_ref[0:1, :] = top
    stat_ref[1:2, :] = total


def row_stats(rot, centroids, scale):
    rows, width = rot.shape
    count = centroids.shape[0]
    tiles = count // TILE
    return pl.pallas_call(
        functools.partial(stats_kernel, scale),
        grid=(tiles,),
        in_specs=[
            pl.BlockSpec((rows, width), lambda i: (0, 0)),
            pl.BlockSpec((TILE, width), lambda i: (i, 0)),
        ],
        out_specs=[
            pl.BlockSpec((TILE, rows), lambda i: (i, 0)),
            pl.BlockSpec((1, 1, rows), lambda i: (i, 0, 0)),
            pl.BlockSpec((2, rows), lambda i: (0, 0)),
        ],
        out_shape=[
            jax.ShapeDtypeStruct((count, rows), f32),
            jax.ShapeDtypeStruct((tiles, 1, rows), f32),
            jax.ShapeDtypeStruct((2, rows), f32),
        ],
        scratch_shapes=[pltpu.VMEM((rows, width), bf16), pltpu.VMEM((8, rows), f32)],
        compiler_params=pltpu.CompilerParams(vmem_limit_bytes=VMEM_BYTES),
        cost_estimate=pl.CostEstimate(
            flops=2 * rows * width * count, bytes_accessed=count * (4 * rows + 2 * width), transcendentals=rows * count
        ),
        name="row_stats",
    )(rot, centroids)


def cross_kernel(tiles, exp_ref, tile_top_ref, stat_ref, cent_ref, emb_ref, cross_ref, acc):
    step = pl.program_id(0)
    factor = jnp.exp(tile_top_ref[0] - stat_ref[0:1, :]) * stat_ref[1:2, :]
    weights = (exp_ref[...] * factor).astype(bf16)
    part = dot(weights, cent_ref[...], 0, 0)

    @pl.when(step == 0)
    def _():
        acc[...] = part

    @pl.when(step > 0)
    def _():
        acc[...] += part

    @pl.when(step == tiles - 1)
    def _():
        rebuilt = acc[...]
        high = rebuilt.astype(bf16)
        low = (rebuilt - high.astype(f32)).astype(bf16)
        emb = emb_ref[...]
        cross_ref[...] = dot(emb, high, 0, 0) + dot(emb, low, 0, 0)


def cross_partial(exps, tile_tops, stats, centroids, embeddings):
    count, rows = exps.shape
    width = centroids.shape[1]
    tiles = count // TILE
    return pl.pallas_call(
        functools.partial(cross_kernel, tiles),
        grid=(tiles,),
        in_specs=[
            pl.BlockSpec((TILE, rows), lambda i: (i, 0)),
            pl.BlockSpec((1, 1, rows), lambda i: (i, 0, 0)),
            pl.BlockSpec((2, rows), lambda i: (0, 0)),
            pl.BlockSpec((TILE, width), lambda i: (i, 0)),
            pl.BlockSpec((rows, width), lambda i: (0, 0)),
        ],
        out_specs=pl.BlockSpec((width, width), lambda i: (0, 0)),
        out_shape=jax.ShapeDtypeStruct((width, width), f32),
        scratch_shapes=[pltpu.VMEM((rows, width), f32)],
        compiler_params=pltpu.CompilerParams(vmem_limit_bytes=VMEM_BYTES),
        cost_estimate=pl.CostEstimate(
            flops=2 * rows * width * count, bytes_accessed=count * (4 * rows + 2 * width), transcendentals=0
        ),
        name="cross_partial",
    )(exps, tile_tops, stats, centroids, embeddings)


def sums_kernel(scale, rows_ref, stat_ref, cent_ref, sums_ref, counts_ref, rows_s):
    @pl.when(pl.program_id(0) == 0)
    def _():
        rows_s[...] = rows_ref[...].astype(bf16)

    cents = cent_ref[0].astype(bf16)
    rot = rows_s[...]
    scores = (dot(cents, rot, 1, 1) - half_norms(cents)) * scale
    weights = (jnp.exp(scores - stat_ref[0:1, :]) * stat_ref[1:2, :]).astype(bf16)
    sums_ref[0] = dot(weights, rot, 1, 0)
    counts = jnp.sum(weights.astype(f32), axis=1, keepdims=True)
    counts_ref[0] = jnp.broadcast_to(counts, counts_ref.shape[1:])


def cent_partial(rows, stats, blocks, scale):
    count, width = rows.shape
    number, block, _ = blocks.shape
    return pl.pallas_call(
        functools.partial(sums_kernel, scale),
        grid=(number,),
        in_specs=[
            pl.BlockSpec((count, width), lambda i: (0, 0)),
            pl.BlockSpec((2, count), lambda i: (0, 0)),
            pl.BlockSpec((1, block, width), lambda i: (i, 0, 0)),
        ],
        out_specs=[
            pl.BlockSpec((1, block, width), lambda i: (i, 0, 0)),
            pl.BlockSpec((1, block, 128), lambda i: (i, 0, 0)),
        ],
        out_shape=[
            jax.ShapeDtypeStruct((number, block, width), f32),
            jax.ShapeDtypeStruct((number, block, 128), f32),
        ],
        scratch_shapes=[pltpu.VMEM((count, width), bf16)],
        compiler_params=pltpu.CompilerParams(vmem_limit_bytes=VMEM_BYTES),
        cost_estimate=pl.CostEstimate(
            flops=4 * count * width * number * block,
            bytes_accessed=8 * number * block * width + 4 * count * width,
            transcendentals=count * number * block,
        ),
        name="cent_partial",
    )(rows, stats, blocks)


def split(value):
    high = value.astype(bf16)
    return high, (value - high.astype(f32)).astype(bf16)


def dot3(a, b, ca, cb):
    return dot(a[0], b[0], ca, cb) + dot(a[0], b[1], ca, cb) + dot(a[1], b[0], ca, cb)


def polar_kernel(cross_ref, out_ref, high_s, low_s, gram_s):
    cross = cross_ref[...]
    unit = cross * lax.rsqrt(jnp.sum(cross * cross, keepdims=True) + EPSILON)
    high, low = split(unit)
    high_s[...] = high
    low_s[...] = low
    gram_once = dot3((high, low), (high, low), 0, 0)
    gram_s[...] = gram_once
    pair = split(gram_once)
    gram_twice = dot3(pair, pair, 1, 0)
    norm_power = jnp.sum(gram_twice * gram_twice, keepdims=True) + EPSILON
    inverse = 1.0 / jnp.sqrt(jnp.sqrt(jnp.sqrt(norm_power)))
    pair = split(gram_s[...] * (inverse * inverse))
    product = dot3((high_s[...], low_s[...]), pair, 1, 0)
    out_ref[...] = (1.5 * unit - 0.5 * product) * inverse

    @pl.loop(1, NS_ITERS)
    def _(_):
        pair = split(out_ref[...])
        inner = split(dot3(pair, pair, 0, 0))
        out_ref[...] = 1.5 * out_ref[...] - 0.5 * dot3(pair, inner, 1, 0)


def polar_update(cross):
    width = cross.shape[0]
    return pl.pallas_call(
        polar_kernel,
        in_specs=[pl.BlockSpec(memory_space=pltpu.VMEM)],
        out_specs=pl.BlockSpec(memory_space=pltpu.VMEM),
        out_shape=jax.ShapeDtypeStruct((width, width), f32),
        scratch_shapes=[
            pltpu.VMEM((width, width), bf16),
            pltpu.VMEM((width, width), bf16),
            pltpu.VMEM((width, width), f32),
        ],
        compiler_params=pltpu.CompilerParams(vmem_limit_bytes=VMEM_BYTES),
        cost_estimate=pl.CostEstimate(flops=54 * width**3, bytes_accessed=8 * width**2, transcendentals=0),
        name="polar_update",
    )(cross)


def solution(mesh):
    dp, cent = mesh.shape["dp"], mesh.shape["cent"]
    across_core = [(i, i ^ 1) for i in range(cent)]
    across_x = [(i, i ^ 2) for i in range(cent)]

    def gather_small(value, axis, size):
        slots = jnp.zeros((size, *value.shape), f32)
        slots = lax.dynamic_update_slice_in_dim(slots, value[None], lax.axis_index(axis), 0)
        return lax.psum(slots, axis)

    def body(embeddings, centroids, rotation):
        rows, width = embeddings.shape
        scale = SHARPNESS / math.sqrt(width)
        share = rows // GROUP
        block = centroids.shape[0] // dp
        dp_index = lax.axis_index("dp")
        cent_index = lax.axis_index("cent")
        first_row = lax.rem(cent_index, GROUP) * share

        rotated = jnp.dot(embeddings.astype(f32), rotation, precision=lax.Precision.HIGHEST)
        rotated = lax.reduce_precision(rotated, 8, 7)

        own_rows = lax.dynamic_slice_in_dim(rotated, first_row, share, 0)
        all_rows = lax.all_gather(own_rows, "dp", axis=0, tiled=True)

        own_block = lax.dynamic_slice_in_dim(centroids, dp_index * block, block, 0)
        own_block = lax.optimization_barrier(own_block.astype(f32))
        x_block = lax.ppermute(own_block, "cent", across_x)
        pair = jnp.stack([own_block, x_block])
        other_pair = lax.ppermute(pair, "cent", across_core)
        blocks = jnp.concatenate([pair, other_pair])

        exps, tile_tops, local = row_stats(rotated, centroids, scale)
        gathered = gather_small(local, "cent", cent)
        top = jnp.max(gathered[:, 0], axis=0)
        total = jnp.sum(gathered[:, 1] * jnp.exp(gathered[:, 0] - top), axis=0)
        stats = jnp.stack([top, 1.0 / total])

        cross = lax.psum(cross_partial(exps, tile_tops, stats, centroids, embeddings), ("dp", "cent"))
        new_rotation = polar_update(cross)

        own_stats = lax.dynamic_slice_in_dim(stats, first_row, share, 1)
        all_stats = gather_small(own_stats, "dp", dp)
        all_stats = jnp.swapaxes(all_stats, 0, 1).reshape(2, dp * share)
        sums, counts = cent_partial(all_rows, all_stats, blocks, scale)
        sums = sums[:2] + lax.ppermute(sums[2:], "cent", across_core)
        counts = counts[..., 0]
        counts = counts[:2] + lax.ppermute(counts[2:], "cent", across_core)
        sums = sums[0] + lax.ppermute(sums[1], "cent", across_x)
        counts = counts[0] + lax.ppermute(counts[1], "cent", across_x)
        new_centroids = (sums + PRIOR_WEIGHT * own_block) / (counts + PRIOR_WEIGHT)[:, None]
        return new_centroids, new_rotation

    in_specs = (P("dp", None), P("cent", None), P())
    out_specs = (P(("cent", "dp"), None), P())
    return jax.shard_map(body, mesh=mesh, in_specs=in_specs, out_specs=out_specs, check_vma=False)
```

time: 415 us -> 357 us (0.86); the launches traced: 409 us -> 357 us
  matrix products: 101 us -> 4.35 us
  Pallas kernels: 0 us -> 95.2 us
  waiting for transfers between devices: 207 us -> 156 us
  local copies, waits for them, and re-layouts: 5.63 us -> 13 us
  other arithmetic: 23.5 us -> 16.5 us
  starting transfers between devices: 0.08 us -> 5.75 us
    dot_general x15 -> x1, matrix products: 101 us -> 4.35 us  [body(): jnp.dot(embeddings.astype(f32), rotation, precision=lax.Precision.HIGHEST)]
    pallas_call x0 -> x4, Pallas kernels: none -> 95.2 us  [the longest x1 48.6 us: polar_update(): pl.pallas_call(polar_kernel, in_specs=[pl.BlockSpec(memory_space=pltpu.VM...]
    psum x1, waiting for transfers between devices: 207 us -> 121 us  [body(): lax.psum(cross_partial(exps, tile_tops, stats, centroids, embeddings), ('...]
    psum x1 -> x2, blocking collectives: 5.92 us -> 49.8 us  [gather_small(): return lax.psum(slots, axis)]
    unnamed x1 -> x0, blocking collectives: 39.7 us -> none
    ppermute x0 -> x6, waiting for transfers between devices: none -> 35.2 us  [the longest x1 34.4 us: body(): x_block = lax.ppermute(own_block, 'cent', across_x)]
    reduce_sum x4 -> x1, other arithmetic: 20.5 us -> 0.02 us  [body(): total = jnp.sum(gathered[:, 1] * jnp.exp(gathered[:, 0] - top), axis=0)]
    pmax x1 -> x0, blocking collectives: 8.31 us -> none  [body(): row_top = lax.pmax(jnp.max(scores, axis=1), 'cent')]
  transfers between devices with their start and end apart: 2 -> 8, of which waited for: 1 -> 3; matrix products, arithmetic and copies ran while one was open for 20% -> 4% of each run, Pallas kernels for 0% -> 22%
where the time goes in v1:
time: 357 us
  waiting for transfers between devices  156 us (44%)
  Pallas kernels  95.2 us (27%)
  blocking collectives  49.8 us (14%)
  other arithmetic  16.5 us (5%)
  between operations  15.6 us (4%)
  local copies, waits for them, and re-layouts  13 us (4%)
  starting transfers between devices  5.75 us (2%)
  matrix products  4.35 us (1%)
    psum x1, waiting for transfers between devices, body(): lax.psum(cross_partial(exps, tile_tops, stats, centroids, embeddings), ('...  121 us
    psum x2, blocking collectives, gather_small(): return lax.psum(slots, axis)  49.8 us
    pallas_call x1, Pallas kernels, polar_update(): pl.pallas_call(polar_kernel, in_specs=[pl.BlockSpec(memory_space=pltpu.VM...  48.6 us
    ppermute x1, waiting for transfers between devices, body(): x_block = lax.ppermute(own_block, 'cent', across_x)  34.4 us
    pallas_call x1, Pallas kernels, cent_partial(): pl.pallas_call(functools.partial(sums_kernel, scale), grid=(number,), in_...  16 us
    pallas_call x1, Pallas kernels, cross_partial(): pl.pallas_call(functools.partial(cross_kernel, tiles), grid=(tiles,), in_...  15.9 us
    pallas_call x1, Pallas kernels, row_stats(): pl.pallas_call(functools.partial(stats_kernel, scale), grid=(tiles,), in_...  14.6 us
  transfers between devices with their start and end apart: 8, of which 3 were waited for; matrix products, arithmetic and copies ran while one was open for 4% of the time, Pallas kernels for 22%

profile of v1, /device:TPU:0, one launch (start us, length us, event | category | flops | bytes accessed | tf_op | source)
XLA Modules:
  0.0 356.7 jit_solution(2731607631130861984)
XLA Ops:
  8.1 1.6 copy-done
  9.7 4.3 %convolution_reduce-precision_fusion.rot_ref = f32[768,768]{1,0:T(8,128)S(1)} fusion(bf16[768,768]{1,0:T(8,128)(2,1)} %emb_ref.1, f32[768,768]{1,0:T(8,128)S(1)} %copy-done), kind=kOutput, calls=%fused_computation.3 | convolution fusion | flops 5436407808 | bytes 5898240 | tf_op jit(solution)/shard_map/dot_general | solution.py:245
  14.0 1.4 copy-done.6
  15.4 0.9 constant_dynamic-slice_fusion
  16.3 0.0 all-reduce.2.cloned.1.call-start
  16.4 1.2 dynamic-slice_convert_fusion
  17.6 3.0 collective-permute-start
  20.6 34.4 %collective-permute-done = f32[512,768]{1,0:T(8,128)S(1)} collective-permute-done((f32[512,768]{1,0:T(8,128)S(1)}, f32[512,768]{1,0:T(8,128)S(1)}, u32[]{:S(2)}, u32[]{:S(2)}) %collective-permute-start) | collective-permute-done | bytes 1572896 | tf_op jit(solution)/shard_map/ppermute | solution.py:253
  55.0 2.2 pad_maximum_fusion.1
  57.3 14.6 %row_stats.1 = (f32[4096,768]{1,0:T(8,128)}, f32[8,1,768]{2,1,0:T(1,128)}, f32[2,768]{1,0:T(2,128)}) custom-call(f32[768,768]{1,0:T(8,128)} %copy-done.6, bf16[4096,768]{1,0:T(8,128)(2,1)} %cent_ref.3), custom_call_target="tpu_custom_call" | custom-call | flops 4831838208 | bytes 18874368 | tf_op jit(solution)/shard_map/row_stats/pallas_call | solution.py:58
  71.9 0.7 bitcast_dynamic-update-slice_fusion
  72.6 12.7 %psum.21 = f32[4,2,768]{2,1,0:T(2,128)S(1)} all-reduce(f32[4,2,768]{2,1,0:T(2,128)S(1)} %bitcast_dynamic-update-slice_fusion), channel_id=1, replica_groups=mesh['dp'=8,'cent'=4] {'cent'}, use_global_device_ids=true, to_apply=%region_0.0 | all-reduce | flops 6144 | bytes 49152 | tf_op jit(solution)/shard_map/psum | solution.py:234
  85.4 0.1 fusion.7
  85.5 0.1 reshape.20
  85.6 37.1 %psum.22.stat_ref = f32[2,1536]{1,0:T(2,128)} all-reduce(f32[2,1536]{1,0:T(2,128)S(1)} %reshape.20), channel_id=1, replica_groups=mesh['dp'=8,'cent'=4] {'dp'}, use_global_device_ids=true, to_apply=%region_3.0 | all-reduce | flops 3072 | bytes 24576 | tf_op jit(solution)/shard_map/psum | solution.py:234
  122.7 5.7 %pad_maximum_fusion.cent_ref = f32[4,512,768]{2,1,0:T(8,128)} fusion(f32[2,512,768]{2,1,0:T(8,128)} %collective-permute-done.1, f32[1,512,768]{2,1,0:T(8,128)} %bitcast.34, f32[1,512,768]{2,1,0:T(8,128)S(1)} %bitcast.32), kind=kLoop, calls=%fused_computation | loop fusion | flops 3145728 | bytes 12582912 | tf_op jit(solution)/shard_map/concatenate | solution.py:256
  128.4 16.0 %cent_partial.1 = (f32[4,512,768]{2,1,0:T(8,128)}, f32[4,512,128]{2,1,0:T(8,128)}) custom-call(f32[1536,768]{1,0:T(8,128)} %all-gather.2.cloned.1.call-done.rows_ref, f32[2,1536]{1,0:T(2,128)} %psum.22.stat_ref, f32[4,512,768]{2,1,0:T(8,128)} %pad_maximum_fusion.cent_ref), custom_call_target="tpu_custom_call" | custom-call | flops 9663676416 | bytes 17301504 | tf_op jit(solution)/shard_map/cent_partial/pallas_call | solution.py:149
  144.4 3.8 %slice.43 = f32[2,512,768]{2,1,0:T(8,128)} slice(f32[4,512,768]{2,1,0:T(8,128)} %get-tuple-element.8), slice={[2:4], [0:512], [0:768]} | slice | bytes 6291456 | tf_op jit(solution)/shard_map/slice | solution.py:271
  148.2 0.6 pad_maximum_fusion.2.stat_ref
  148.9 15.9 %cross_partial.1 = f32[768,768]{1,0:T(8,128)} custom-call(f32[4096,768]{1,0:T(8,128)} %get-tuple-element.10.exp_ref, f32[8,1,768]{2,1,0:T(1,128)} %get-tuple-element.11.tile_top_ref, f32[2,768]{1,0:T(2,128)} %pad_maximum_fusion.2.stat_ref, bf16[4096,768]{1,0:T(8,128)(2,1)} %cent_ref.3, bf16[768,768]{1,0:T(8,128)(2,1)} %emb_ref.1), custom_call_target="tpu_custom_call" | custom-call | flops 4831838208 | bytes 18874368 | tf_op jit(solution)/shard_map/cross_partial/pallas_call | solution.py:111
  164.8 1.2 copy-done.7
  166.0 0.3 slice_reduce_fusion
  166.4 0.6 collective-permute-start.4
  166.9 0.8 collective-permute-done.4
  167.8 0.6 collective-permute-start.5
  168.4 3.2 slice_add_fusion
  171.7 1.7 copy-done.3
  173.3 1.2 slice_bitcast_fusion
  174.6 1.5 collective-permute-start.3
  176.0 121.1 %all-reduce.2.cloned.1.call-done.cross_ref = f32[768,768]{1,0:T(8,128)} async-done(((f32[768,768]{1,0:T(8,128)}), f32[768,768]{1,0:T(8,128)}) %all-reduce.2.cloned.1.call-update) | async-done | bytes 2359312 | tf_op jit(solution)/shard_map/psum | solution.py:264
  297.1 48.6 %polar_update.1 = f32[768,768]{1,0:T(8,128)} custom-call(f32[768,768]{1,0:T(8,128)} %all-reduce.2.cloned.1.call-done.cross_ref), custom_call_target="tpu_custom_call" | custom-call | flops 24461180928 | bytes 4718592 | tf_op jit(solution)/shard_map/polar_update/pallas_call | solution.py:210
  345.8 3.4 fusion.2
  (34 shorter events, 0.2 us)
Async XLA Ops:
  8.0 1.7 copy-start
  8.0 120.4 %all-gather.2.cloned.1.call-start = ((), (), s32[]{:S(2)}) async-start(), calls=%async_computation | async-start | bytes 5308416 | tf_op jit(solution)/shard_map/all_gather | solution.py:249
  14.0 1.4 copy-start.6
  16.3 280.8 %all-reduce.2.cloned.1.call-start = ((), (), s32[]{:S(2)}) async-start(), calls=%async_computation.1 | async-start | bytes 4718592 | tf_op jit(solution)/shard_map/psum | solution.py:264
  17.6 105.1 %copy-start.2 = (f32[512,768]{1,0:T(8,128)}, f32[512,768]{1,0:T(8,128)S(1)}, u32[]{:S(2)}) copy-start(f32[512,768]{1,0:T(8,128)S(1)} %dynamic-slice_convert_fusion) | copy-start | bytes 4718596
  17.6 37.4 %collective-permute-start = (f32[512,768]{1,0:T(8,128)S(1)}, f32[512,768]{1,0:T(8,128)S(1)}, u32[]{:S(2)}, u32[]{:S(2)}) collective-permute-start(f32[512,768]{1,0:T(8,128)S(1)} %dynamic-slice_convert_fusion), channel_id=1, source_target_pairs={{0,2},{1,3},{2,0},{3,1},{4,6},{5,7},{6,4},{7,5},{8,10},{9,11},{10,... | collective-permute-start | bytes 4718600 | tf_op jit(solution)/shard_map/ppermute | solution.py:253
  55.0 2.2 copy-start.5
  57.3 65.4 %collective-permute-start.1 = (f32[2,512,768]{2,1,0:T(8,128)}, f32[2,512,768]{2,1,0:T(8,128)}, u32[]{:S(2)}, u32[]{:S(2)}) collective-permute-start(f32[2,512,768]{2,1,0:T(8,128)} %pad_maximum_fusion.1), channel_id=1, source_target_pairs={{0,1},{1,0},{2,3},{3,2},{4,5},{5,4},{6,7},{7,6},{8,9},{9,8},{10,11... | collective-permute-start | bytes 9437192 | tf_op jit(solution)/shard_map/ppermute | solution.py:255
  148.2 20.2 %collective-permute-start.2 = (f32[2,512,768]{2,1,0:T(8,128)}, f32[2,512,768]{2,1,0:T(8,128)}, u32[]{:S(2)}, u32[]{:S(2)}) collective-permute-start(f32[2,512,768]{2,1,0:T(8,128)} %slice.43), channel_id=1, source_target_pairs={{0,1},{1,0},{2,3},{3,2},{4,5},{5,4},{6,7},{7,6},{8,9},{9,8},{10,11... | collective-permute-start | bytes 9437192 | tf_op jit(solution)/shard_map/ppermute | solution.py:271
  164.8 1.2 copy-start.7
  166.4 1.4 collective-permute-start.4
  167.8 178.0 %collective-permute-start.5 = (f32[512]{0:T(512)S(1)}, f32[512]{0:T(512)S(1)}, u32[]{:S(2)}, u32[]{:S(2)}) collective-permute-start(f32[512]{0:T(512)S(1)} %bitcast.37), channel_id=1, source_target_pairs={{0,2},{1,3},{2,0},{3,1},{4,6},{5,7},{6,4},{7,5},{8,10},{9,11},{10,... | collective-permute-start | bytes 6152 | tf_op jit(solution)/shard_map/ppermute | solution.py:275
  171.6 1.7 copy-start.3
  174.6 171.2 %collective-permute-start.3 = (f32[512,768]{1,0:T(8,128)}, f32[512,768]{1,0:T(8,128)}, u32[]{:S(2)}, u32[]{:S(2)}) collective-permute-start(f32[512,768]{1,0:T(8,128)} %slice_bitcast_fusion), channel_id=1, source_target_pairs={{0,2},{1,3},{2,0},{3,1},{4,6},{5,7},{6,4},{7,5},{8,10},{9,11},{10,... | collective-permute-start | bytes 4718600 | tf_op jit(solution)/shard_map/ppermute | solution.py:274
  297.1 48.6 %copy-start.4 = (f32[2,512,768]{2,1,0:T(8,128)S(1)}, f32[2,512,768]{2,1,0:T(8,128)}, u32[]{:S(2)}) copy-start(f32[2,512,768]{2,1,0:T(8,128)} %copy-done.3) | copy-start | bytes 9437188
  345.8 3.5 copy-start.1
Sparse Core Ops, SparseCore 0:
  16.4 82.7 all-gather.1
Sparse Core Ops, SparseCore 1:
  164.9 132.2 all-reduce.1

commit v2 on v1

--- a/solution.py
+++ b/solution.py
@@ -173,36 +173,24 @@
     )(rows, stats, blocks)
 
 
-def split(value):
-    high = value.astype(bf16)
-    return high, (value - high.astype(f32)).astype(bf16)
-
-
-def dot3(a, b, ca, cb):
-    return dot(a[0], b[0], ca, cb) + dot(a[0], b[1], ca, cb) + dot(a[1], b[0], ca, cb)
-
-
-def polar_kernel(cross_ref, out_ref, high_s, low_s, gram_s):
+def polar_kernel(cross_ref, out_ref, half_s):
     cross = cross_ref[...]
     unit = cross * lax.rsqrt(jnp.sum(cross * cross, keepdims=True) + EPSILON)
-    high, low = split(unit)
-    high_s[...] = high
-    low_s[...] = low
-    gram_once = dot3((high, low), (high, low), 0, 0)
-    gram_s[...] = gram_once
-    pair = split(gram_once)
-    gram_twice = dot3(pair, pair, 1, 0)
+    half = unit.astype(bf16)
+    half_s[...] = half
+    gram_once = dot(half, half, 0, 0)
+    gram_half = gram_once.astype(bf16)
+    gram_twice = dot(gram_half, gram_half, 1, 0)
     norm_power = jnp.sum(gram_twice * gram_twice, keepdims=True) + EPSILON
     inverse = 1.0 / jnp.sqrt(jnp.sqrt(jnp.sqrt(norm_power)))
-    pair = split(gram_s[...] * (inverse * inverse))
-    product = dot3((high_s[...], low_s[...]), pair, 1, 0)
+    product = dot(half_s[...], gram_half, 1, 0) * (inverse * inverse)
     out_ref[...] = (1.5 * unit - 0.5 * product) * inverse
 
     @pl.loop(1, NS_ITERS)
     def _(_):
-        pair = split(out_ref[...])
-        inner = split(dot3(pair, pair, 0, 0))
-        out_ref[...] = 1.5 * out_ref[...] - 0.5 * dot3(pair, inner, 1, 0)
+        half_s[...] = out_ref[...].astype(bf16)
+        inner = dot(half_s[...], half_s[...], 0, 0).astype(bf16)
+        out_ref[...] = 1.5 * out_ref[...] - 0.5 * dot(half_s[...], inner, 1, 0)
 
 
 def polar_update(cross):
@@ -214,24 +202,56 @@
         out_shape=jax.ShapeDtypeStruct((width, width), f32),
         scratch_shapes=[
             pltpu.VMEM((width, width), bf16),
-            pltpu.VMEM((width, width), bf16),
-            pltpu.VMEM((width, width), f32),
         ],
         compiler_params=pltpu.CompilerParams(vmem_limit_bytes=VMEM_BYTES),
-        cost_estimate=pl.CostEstimate(flops=54 * width**3, bytes_accessed=8 * width**2, transcendentals=0),
+        cost_estimate=pl.CostEstimate(flops=18 * width**3, bytes_accessed=8 * width**2, transcendentals=0),
         name="polar_update",
     )(cross)
 
 
 def solution(mesh):
     dp, cent = mesh.shape["dp"], mesh.shape["cent"]
-    across_core = [(i, i ^ 1) for i in range(cent)]
-    across_x = [(i, i ^ 2) for i in range(cent)]
-
-    def gather_small(value, axis, size):
-        slots = jnp.zeros((size, *value.shape), f32)
-        slots = lax.dynamic_update_slice_in_dim(slots, value[None], lax.axis_index(axis), 0)
-        return lax.psum(slots, axis)
+    sizes = {"dp": dp, "cent": cent}
+    cent_bits = [1 << k for k in range(cent.bit_length() - 1)]
+    dp_bits = [1 << k for k in range(dp.bit_length() - 1)]
+
+    def swap(value, axis, bit):
+        return lax.ppermute(value, axis, [(i, i ^ bit) for i in range(sizes[axis])])
+
+    def is_upper(axis, bit):
+        return lax.rem(lax.div(lax.axis_index(axis), bit), 2)
+
+    def halve(value, axis, bit):
+        side, half = is_upper(axis, bit), value.shape[0] // 2
+        sent = lax.dynamic_slice_in_dim(value, (1 - side) * half, half, 0)
+        kept = lax.dynamic_slice_in_dim(value, side * half, half, 0)
+        return kept + swap(sent, axis, bit)
+
+    def double(value, axis, bit):
+        other = swap(value, axis, bit)
+        upper = is_upper(axis, bit) == 1
+        return jnp.concatenate([jnp.where(upper, other, value), jnp.where(upper, value, other)])
+
+    def after(value, earlier):
+        return lax.optimization_barrier((value, earlier))[0]
+
+    def sum_part(value, halved, added, earlier):
+        for axis, bit in halved:
+            value = halve(value, axis, bit)
+        for axis, bit in added:
+            value = value + swap(value, axis, bit)
+        value = after(value, earlier)
+        for axis, bit in reversed(halved):
+            value = double(value, axis, bit)
+        return value
+
+    def sum_everywhere(value, earlier):
+        value = halve(value, "cent", 1)
+        rows = value.shape[0] // 2
+        rest = [("dp", bit) for bit in dp_bits[1:]] + [("cent", bit) for bit in cent_bits[2:]]
+        first = sum_part(value[:rows], [("cent", 2), ("dp", 1)], rest, earlier)
+        second = sum_part(value[rows:], [("dp", 1), ("cent", 2)], rest, earlier)
+        return double(jnp.concatenate([first, second]), "cent", 1)
 
     def body(embeddings, centroids, rotation):
         rows, width = embeddings.shape
@@ -246,33 +266,39 @@
         rotated = lax.reduce_precision(rotated, 8, 7)
 
         own_rows = lax.dynamic_slice_in_dim(rotated, first_row, share, 0)
+        own_rows = lax.optimization_barrier(own_rows)
         all_rows = lax.all_gather(own_rows, "dp", axis=0, tiled=True)
 
         own_block = lax.dynamic_slice_in_dim(centroids, dp_index * block, block, 0)
         own_block = lax.optimization_barrier(own_block.astype(f32))
-        x_block = lax.ppermute(own_block, "cent", across_x)
-        pair = jnp.stack([own_block, x_block])
-        other_pair = lax.ppermute(pair, "cent", across_core)
+        x_block = swap(own_block, "cent", 2)
+
+        exps, tile_tops, local = row_stats(after(rotated, own_rows), centroids, scale)
+        top, total = local[:1], local[1:]
+        for bit in cent_bits:
+            other = swap(jnp.concatenate([top, total]), "cent", bit)
+            new_top = jnp.maximum(top, other[:1])
+            total = total * jnp.exp(top - new_top) + other[1:] * jnp.exp(other[:1] - new_top)
+            top = new_top
+        stats = jnp.concatenate([top, 1.0 / total])
+
+        partial = cross_partial(exps, tile_tops, stats, centroids, embeddings)
+        cross = sum_everywhere(partial, all_rows)
+
+        pair = jnp.stack([own_block, after(x_block, partial)])
+        other_pair = swap(pair, "cent", 1)
         blocks = jnp.concatenate([pair, other_pair])
-
-        exps, tile_tops, local = row_stats(rotated, centroids, scale)
-        gathered = gather_small(local, "cent", cent)
-        top = jnp.max(gathered[:, 0], axis=0)
-        total = jnp.sum(gathered[:, 1] * jnp.exp(gathered[:, 0] - top), axis=0)
-        stats = jnp.stack([top, 1.0 / total])
-
-        cross = lax.psum(cross_partial(exps, tile_tops, stats, centroids, embeddings), ("dp", "cent"))
-        new_rotation = polar_update(cross)
-
-        own_stats = lax.dynamic_slice_in_dim(stats, first_row, share, 1)
-        all_stats = gather_small(own_stats, "dp", dp)
+        all_stats = after(lax.dynamic_slice_in_dim(stats, first_row, share, 1), partial)[None]
+        for bit in dp_bits:
+            all_stats = double(all_stats, "dp", bit)
         all_stats = jnp.swapaxes(all_stats, 0, 1).reshape(2, dp * share)
-        sums, counts = cent_partial(all_rows, all_stats, blocks, scale)
-        sums = sums[:2] + lax.ppermute(sums[2:], "cent", across_core)
+        sums, counts = cent_partial(all_rows, after(all_stats, cross), blocks, scale)
+        new_rotation = polar_update(after(cross, counts))
+        sums = sums[:2] + swap(sums[2:], "cent", 1)
         counts = counts[..., 0]
-        counts = counts[:2] + lax.ppermute(counts[2:], "cent", across_core)
-        sums = sums[0] + lax.ppermute(sums[1], "cent", across_x)
-        counts = counts[0] + lax.ppermute(counts[1], "cent", across_x)
+        counts = counts[:2] + swap(counts[2:], "cent", 1)
+        sums = sums[0] + swap(sums[1], "cent", 2)
+        counts = counts[0] + swap(counts[1], "cent", 2)
         new_centroids = (sums + PRIOR_WEIGHT * own_block) / (counts + PRIOR_WEIGHT)[:, None]
         return new_centroids, new_rotation
 

time: 357 us -> 234 us (0.66)
  waiting for transfers between devices: 156 us -> 94.1 us
  blocking collectives: 49.8 us -> 0 us
  Pallas kernels: 95.2 us -> 60.4 us
  starting transfers between devices: 5.75 us -> 28.8 us
  other arithmetic: 16.5 us -> 21.3 us
    psum x1 -> x0, waiting for transfers between devices: 121 us -> none  [body(): lax.psum(cross_partial(exps, tile_tops, stats, centroids, embeddings), ('...]
    ppermute x6 -> x25, waiting for transfers between devices: 35.2 us -> 94 us  [swap(): return lax.ppermute(value, axis, [(i, i ^ bit) for i in range(sizes[axis])])]
    psum x2 -> x0, blocking collectives: 49.8 us -> none  [gather_small(): return lax.psum(slots, axis)]
    pallas_call x1, Pallas kernels: 48.6 us -> 13.5 us  [polar_update(): pl.pallas_call(polar_kernel, in_specs=[pl.BlockSpec(memory_space=pltpu.VM...]
    ppermute x6 -> x25, starting transfers between devices: 5.66 us -> 28.8 us  [swap(): return lax.ppermute(value, axis, [(i, i ^ bit) for i in range(sizes[axis])])]
  transfers between devices with their start and end apart: 8 -> 26, of which waited for: 3 -> 16; matrix products, arithmetic and copies ran while one was open for 4% -> 8% of each run, Pallas kernels for 22% -> 19%
where the time goes in v2:
time: 234 us; the launch traced here: 233 us
  waiting for transfers between devices  94.1 us (40%)
  Pallas kernels  60.4 us (26%)
  starting transfers between devices  28.8 us (12%)
  other arithmetic  21.3 us (9%)
  between operations  14.3 us (6%)
  local copies, waits for them, and re-layouts  9.59 us (4%)
  matrix products  4.35 us (2%)
    ppermute x25, waiting for transfers between devices, swap(): return lax.ppermute(value, axis, [(i, i ^ bit) for i in range(sizes[axis])])  94 us
    ppermute x25, starting transfers between devices, swap(): return lax.ppermute(value, axis, [(i, i ^ bit) for i in range(sizes[axis])])  28.8 us
    pallas_call x1, Pallas kernels, cent_partial(): pl.pallas_call(functools.partial(sums_kernel, scale), grid=(number,), in_...  16.1 us
    pallas_call x1, Pallas kernels, cross_partial(): pl.pallas_call(functools.partial(cross_kernel, tiles), grid=(tiles,), in_...  16 us
    pallas_call x1, Pallas kernels, row_stats(): pl.pallas_call(functools.partial(stats_kernel, scale), grid=(tiles,), in_...  14.8 us
    pallas_call x1, Pallas kernels, polar_update(): pl.pallas_call(polar_kernel, in_specs=[pl.BlockSpec(memory_space=pltpu.VM...  13.5 us
    concatenate x1, other arithmetic, body(): blocks = jnp.concatenate([pair, other_pair])  5.63 us
  transfers between devices with their start and end apart: 26, of which 16 were waited for; matrix products, arithmetic and copies ran while one was open for 8% of the time, Pallas kernels for 19%

profile of v2, /device:TPU:0, one launch (start us, length us, event | category | flops | bytes accessed | tf_op | source)
XLA Modules:
  0.0 232.7 jit_solution(15883424195995889109)
XLA Ops:
  7.2 1.6 copy-done
  8.8 4.3 %convolution_reduce-precision_fusion.rot_ref = f32[768,768]{1,0:T(8,128)S(1)} fusion(bf16[768,768]{1,0:T(8,128)(2,1)} %emb_ref.1, f32[768,768]{1,0:T(8,128)S(1)} %copy-done), kind=kOutput, calls=%fused_computation.4 | convolution fusion | flops 5436407808 | bytes 5898240 | tf_op jit(solution)/shard_map/dot_general | solution.py:265
  15.5 14.8 %row_stats.1 = (f32[4096,768]{1,0:T(8,128)}, f32[8,1,768]{2,1,0:T(1,128)}, f32[2,768]{1,0:T(2,128)}) custom-call(f32[768,768]{1,0:T(8,128)} %copy-done.5, bf16[4096,768]{1,0:T(8,128)(2,1)} %cent_ref.3), custom_call_target="tpu_custom_call" | custom-call | flops 4831838208 | bytes 18874368 | tf_op jit(solution)/shard_map/row_stats/pallas_call | solution.py:58
  32.6 2.9 %collective-permute-start.1 = (f32[2,768]{1,0:T(2,128)S(1)}, f32[2,768]{1,0:T(2,128)S(1)}, u32[]{:S(2)}, u32[]{:S(2)}) collective-permute-start(f32[2,768]{1,0:T(2,128)S(1)} %pad_maximum_fusion.8), channel_id=1, source_target_pairs={{0,2},{1,3},{2,0},{3,1},{4,6},{5,7},{6,4},{7,5},{8,10},{9,11},{10,... | collective-permute-start | bytes 18440 | tf_op jit(solution)/shard_map/ppermute | solution.py:219
  35.5 1.6 collective-permute-done.1
  37.7 16.0 %cross_partial.1 = f32[768,768]{1,0:T(8,128)} custom-call(f32[4096,768]{1,0:T(8,128)} %get-tuple-element.16.exp_ref, f32[8,1,768]{2,1,0:T(1,128)} %get-tuple-element.17.tile_top_ref, f32[2,768]{1,0:T(2,128)} %pad_maximum_fusion.7.stat_ref, bf16[4096,768]{1,0:T(8,128)(2,1)} %cent_ref.3, bf16[768,768]{1,0:T(8,128)(2,1)} %emb_ref.1), custom_call_target="tpu_custom_call" | custom-call | flops 4831838208 | bytes 18874368 | tf_op jit(solution)/shard_map/cross_partial/pallas_call | solution.py:111
  53.8 1.6 constant_dynamic-slice_fusion.4
  56.7 2.0 collective-permute-start.19
  58.7 1.8 dynamic-slice_add_fusion
  60.6 1.7 collective-permute-start.6
  63.9 36.2 %collective-permute-done.6 = f32[96,768]{1,0:T(8,128)S(1)} collective-permute-done((f32[96,768]{1,0:T(8,128)S(1)}, f32[96,768]{1,0:T(8,128)S(1)}, u32[]{:S(2)}, u32[]{:S(2)}) %collective-permute-start.6) | collective-permute-done | bytes 294944 | tf_op jit(solution)/shard_map/ppermute | solution.py:219
  100.2 1.8 collective-permute-start.7
  103.6 3.3 %pad_maximum_fusion.1 = f32[2,512,768]{2,1,0:T(8,128)} fusion(f32[1,512,768]{2,1,0:T(8,128)} %bitcast.3, f32[1,512,768]{2,1,0:T(8,128)S(1)} %bitcast.21), kind=kLoop, calls=%fused_computation.1 | loop fusion | flops 786432 | bytes 6291456 | tf_op jit(solution)/shard_map/stack | solution.py:288
  107.0 1.6 collective-permute-start.8
  109.1 4.5 %collective-permute-done.8 = f32[48,768]{1,0:T(8,128)S(1)} collective-permute-done((f32[48,768]{1,0:T(8,128)S(1)}, f32[48,768]{1,0:T(8,128)S(1)}, u32[]{:S(2)}, u32[]{:S(2)}) %collective-permute-start.8) | collective-permute-done | bytes 147488 | tf_op jit(solution)/shard_map/ppermute | solution.py:219
  113.7 2.6 %collective-permute-start.9 = (f32[48,768]{1,0:T(8,128)S(1)}, f32[48,768]{1,0:T(8,128)S(1)}, u32[]{:S(2)}, u32[]{:S(2)}) collective-permute-start(f32[48,768]{1,0:T(8,128)S(1)} %add.103), channel_id=1, source_target_pairs={{0,16},{4,20},{8,24},{12,28},{16,0},{20,4},{24,8},{28,12},{1,17},{... | collective-permute-start | bytes 442376 | tf_op jit(solution)/shard_map/ppermute | solution.py:219
  116.5 3.0 %collective-permute-start.15 = (f32[48,768]{1,0:T(8,128)S(1)}, f32[48,768]{1,0:T(8,128)S(1)}, u32[]{:S(2)}, u32[]{:S(2)}) collective-permute-start(f32[48,768]{1,0:T(8,128)S(1)} %add.111), channel_id=1, source_target_pairs={{0,16},{4,20},{8,24},{12,28},{16,0},{20,4},{24,8},{28,12},{1,17},{... | collective-permute-start | bytes 442376 | tf_op jit(solution)/shard_map/ppermute | solution.py:219
  119.4 7.9 %collective-permute-done.9 = f32[48,768]{1,0:T(8,128)S(1)} collective-permute-done((f32[48,768]{1,0:T(8,128)S(1)}, f32[48,768]{1,0:T(8,128)S(1)}, u32[]{:S(2)}, u32[]{:S(2)}) %collective-permute-start.9) | collective-permute-done | bytes 147488 | tf_op jit(solution)/shard_map/ppermute | solution.py:219
  129.8 2.8 %collective-permute-done.10 = f32[48,768]{1,0:T(8,128)S(1)} collective-permute-done((f32[48,768]{1,0:T(8,128)S(1)}, f32[48,768]{1,0:T(8,128)S(1)}, u32[]{:S(2)}, u32[]{:S(2)}) %collective-permute-start.10) | collective-permute-done | bytes 147488 | tf_op jit(solution)/shard_map/ppermute | solution.py:219
  133.1 3.0 %collective-permute-done.16 = f32[48,768]{1,0:T(8,128)S(1)} collective-permute-done((f32[48,768]{1,0:T(8,128)S(1)}, f32[48,768]{1,0:T(8,128)S(1)}, u32[]{:S(2)}, u32[]{:S(2)}) %collective-permute-start.16) | collective-permute-done | bytes 147488 | tf_op jit(solution)/shard_map/ppermute | solution.py:219
  138.3 1.9 collective-permute-done.11
  140.3 2.6 %collective-permute-done.17 = f32[96,768]{1,0:T(8,128)S(1)} collective-permute-done((f32[96,768]{1,0:T(8,128)S(1)}, f32[96,768]{1,0:T(8,128)S(1)}, u32[]{:S(2)}, u32[]{:S(2)}) %collective-permute-start.17) | collective-permute-done | bytes 294944 | tf_op jit(solution)/shard_map/ppermute | solution.py:219
  145.1 2.6 %collective-permute-done.3 = f32[2,2,192]{2,1,0:T(2,128)S(1)} collective-permute-done((f32[2,2,192]{2,1,0:T(2,128)S(1)}, f32[2,2,192]{2,1,0:T(2,128)S(1)}, u32[]{:S(2)}, u32[]{:S(2)}) %collective-permute-start.3) | collective-permute-done | bytes 3104 | tf_op jit(solution)/shard_map/ppermute | solution.py:219
  147.8 2.4 %collective-permute-start.4 = (f32[4,2,192]{2,1,0:T(2,128)S(1)}, f32[4,2,192]{2,1,0:T(2,128)S(1)}, u32[]{:S(2)}, u32[]{:S(2)}) collective-permute-start(f32[4,2,192]{2,1,0:T(2,128)S(1)} %pad_maximum_fusion.6), channel_id=1, source_target_pairs={{0,16},{4,20},{8,24},{12,28},{16,0},{20,4},{24,8},{28,12},{1,17},{... | collective-permute-start | bytes 18440 | tf_op jit(solution)/shard_map/ppermute | solution.py:219
  150.2 2.2 collective-permute-done.4
  153.1 5.6 %pad_maximum_fusion.cent_ref = f32[4,512,768]{2,1,0:T(8,128)} fusion(f32[2,512,768]{2,1,0:T(8,128)} %collective-permute-done.20, f32[1,512,768]{2,1,0:T(8,128)} %bitcast.3, f32[1,512,768]{2,1,0:T(8,128)S(1)} %bitcast.22), kind=kLoop, calls=%fused_computation | loop fusion | flops 3145728 | bytes 12582912 | tf_op jit(solution)/shard_map/concatenate | solution.py:290
  161.7 16.1 %cent_partial.1 = (f32[4,512,768]{2,1,0:T(8,128)}, f32[4,512,128]{2,1,0:T(8,128)}) custom-call(f32[1536,768]{1,0:T(8,128)} %all-gather.2.cloned.1.call-done.rows_ref, f32[2,1536]{1,0:T(2,128)} %reshape.10.stat_ref, f32[4,512,768]{2,1,0:T(8,128)} %pad_maximum_fusion.cent_ref), custom_call_target="tpu_custom_call" | custom-call | flops 9663676416 | bytes 17301504 | tf_op jit(solution)/shard_map/cent_partial/pallas_call | solution.py:149
  177.8 2.2 slice.69
  180.1 5.6 %collective-permute-done.21 = f32[2,512,768]{2,1,0:T(8,128)S(1)} collective-permute-done((f32[2,512,768]{2,1,0:T(8,128)S(1)}, f32[2,512,768]{2,1,0:T(8,128)S(1)}, u32[]{:S(2)}, u32[]{:S(2)}) %collective-permute-start.21) | collective-permute-done | bytes 3145760 | tf_op jit(solution)/shard_map/ppermute | solution.py:219
  190.1 13.5 %polar_update.1 = f32[768,768]{1,0:T(8,128)} custom-call(f32[768,768]{1,0:T(8,128)} %pad_maximum_fusion.2.cross_ref), custom_call_target="tpu_custom_call" | custom-call | flops 8153726976 | bytes 4718592 | tf_op jit(solution)/shard_map/polar_update/pallas_call | solution.py:198
  203.5 19.4 %collective-permute-done.24 = f32[512]{0:T(512)S(1)} collective-permute-done((f32[512]{0:T(512)S(1)}, f32[512]{0:T(512)S(1)}, u32[]{:S(2)}, u32[]{:S(2)}) %collective-permute-start.24) | collective-permute-done | bytes 2080 | tf_op jit(solution)/shard_map/ppermute | solution.py:219
  222.9 2.9 %fusion.2 = f32[512,768]{1,0:T(8,128)} fusion(f32[512,768]{1,0:T(8,128)} %collective-permute-done.22, f32[2,512,768]{2,1,0:T(8,128)S(1)} %slice_add_fusion, f32[512,768]{1,0:T(8,128)S(1)} %copy-done.3, f32[512]{0:T(512)S(1)} %add_add_fusion), kind=kLoop, calls=%fused_computation.9 | loop fusion | flops 1572864 | bytes 6293504 | tf_op jit(solution)/shard_map/div | solution.py:302
  (89 shorter events, 26.2 us)
Async XLA Ops:
  7.2 1.7 copy-start
  7.2 120.2 %all-gather.2.cloned.1.call-start = ((), (), s32[]{:S(2)}) async-start(), calls=%async_computation | async-start | bytes 5308416 | tf_op jit(solution)/shard_map/all_gather | solution.py:270
  13.2 1.4 copy-start.5
  30.3 1.5 collective-permute-start
  32.6 4.5 %collective-permute-start.1 = (f32[2,768]{1,0:T(2,128)S(1)}, f32[2,768]{1,0:T(2,128)S(1)}, u32[]{:S(2)}, u32[]{:S(2)}) collective-permute-start(f32[2,768]{1,0:T(2,128)S(1)} %pad_maximum_fusion.8), channel_id=1, source_target_pairs={{0,2},{1,3},{2,0},{3,1},{4,6},{5,7},{6,4},{7,5},{8,10},{9,11},{10,... | collective-permute-start | bytes 18440 | tf_op jit(solution)/shard_map/ppermute | solution.py:219
  55.4 3.4 %collective-permute-start.5 = (f32[384,768]{1,0:T(8,128)S(1)}, f32[384,768]{1,0:T(8,128)}, u32[]{:S(2)}, u32[]{:S(2)}) collective-permute-start(f32[384,768]{1,0:T(8,128)S(1)} %constant_dynamic-slice_fusion.4), channel_id=1, source_target_pairs={{0,1},{1,0},{2,3},{3,2},{4,5},{5,4},{6,7},{7,6},{8,9},{9,8},{10,11... | collective-permute-start | bytes 3538952 | tf_op jit(solution)/shard_map/ppermute | solution.py:219
  56.7 96.4 %copy-start.2 = (f32[512,768]{1,0:T(8,128)}, f32[512,768]{1,0:T(8,128)S(1)}, u32[]{:S(2)}) copy-start(f32[512,768]{1,0:T(8,128)S(1)} %dynamic-slice_convert_fusion) | copy-start | bytes 4718596
  56.7 46.9 %collective-permute-start.19 = (f32[512,768]{1,0:T(8,128)S(1)}, f32[512,768]{1,0:T(8,128)}, u32[]{:S(2)}, u32[]{:S(2)}) collective-permute-start(f32[512,768]{1,0:T(8,128)S(1)} %dynamic-slice_convert_fusion), channel_id=1, source_target_pairs={{0,2},{1,3},{2,0},{3,1},{4,6},{5,7},{6,4},{7,5},{8,10},{9,11},{10,... | collective-permute-start | bytes 4718600 | tf_op jit(solution)/shard_map/ppermute | solution.py:219
  60.6 39.5 %collective-permute-start.6 = (f32[96,768]{1,0:T(8,128)S(1)}, f32[96,768]{1,0:T(8,128)S(1)}, u32[]{:S(2)}, u32[]{:S(2)}) collective-permute-start(f32[96,768]{1,0:T(8,128)S(1)} %constant_dynamic-slice_fusion.3), channel_id=1, source_target_pairs={{0,2},{1,3},{2,0},{3,1},{4,6},{5,7},{6,4},{7,5},{8,10},{9,11},{10,... | collective-permute-start | bytes 884744 | tf_op jit(solution)/shard_map/ppermute | solution.py:219
  62.4 39.6 %collective-permute-start.12 = (f32[96,768]{1,0:T(8,128)S(1)}, f32[96,768]{1,0:T(8,128)S(1)}, u32[]{:S(2)}, u32[]{:S(2)}) collective-permute-start(f32[96,768]{1,0:T(8,128)S(1)} %constant_dynamic-slice_fusion.1), channel_id=1, source_target_pairs={{0,4},{4,0},{8,12},{12,8},{16,20},{20,16},{24,28},{28,24},{1,5},{5... | collective-permute-start | bytes 884744 | tf_op jit(solution)/shard_map/ppermute | solution.py:219
  100.2 6.8 %collective-permute-start.7 = (f32[48,768]{1,0:T(8,128)S(1)}, f32[48,768]{1,0:T(8,128)S(1)}, u32[]{:S(2)}, u32[]{:S(2)}) collective-permute-start(f32[48,768]{1,0:T(8,128)S(1)} %constant_dynamic-slice_fusion.2), channel_id=1, source_target_pairs={{0,4},{4,0},{8,12},{12,8},{16,20},{20,16},{24,28},{28,24},{1,5},{5... | collective-permute-start | bytes 442376 | tf_op jit(solution)/shard_map/ppermute | solution.py:219
  102.1 6.5 %collective-permute-start.13 = (f32[48,768]{1,0:T(8,128)S(1)}, f32[48,768]{1,0:T(8,128)S(1)}, u32[]{:S(2)}, u32[]{:S(2)}) collective-permute-start(f32[48,768]{1,0:T(8,128)S(1)} %constant_dynamic-slice_fusion), channel_id=1, source_target_pairs={{0,2},{1,3},{2,0},{3,1},{4,6},{5,7},{6,4},{7,5},{8,10},{9,11},{10,... | collective-permute-start | bytes 442376 | tf_op jit(solution)/shard_map/ppermute | solution.py:219
  106.9 46.2 %collective-permute-start.20 = (f32[2,512,768]{2,1,0:T(8,128)}, f32[2,512,768]{2,1,0:T(8,128)}, u32[]{:S(2)}, u32[]{:S(2)}) collective-permute-start(f32[2,512,768]{2,1,0:T(8,128)} %pad_maximum_fusion.1), channel_id=1, source_target_pairs={{0,1},{1,0},{2,3},{3,2},{4,5},{5,4},{6,7},{7,6},{8,9},{9,8},{10,11... | collective-permute-start | bytes 9437192 | tf_op jit(solution)/shard_map/ppermute | solution.py:219
  107.0 6.7 %collective-permute-start.8 = (f32[48,768]{1,0:T(8,128)S(1)}, f32[48,768]{1,0:T(8,128)S(1)}, u32[]{:S(2)}, u32[]{:S(2)}) collective-permute-start(f32[48,768]{1,0:T(8,128)S(1)} %dynamic-slice_add_fusion.4), channel_id=1, source_target_pairs={{0,8},{4,12},{8,0},{12,4},{16,24},{20,28},{24,16},{28,20},{1,9},{5... | collective-permute-start | bytes 442376 | tf_op jit(solution)/shard_map/ppermute | solution.py:219
  108.6 7.8 %collective-permute-start.14 = (f32[48,768]{1,0:T(8,128)S(1)}, f32[48,768]{1,0:T(8,128)S(1)}, u32[]{:S(2)}, u32[]{:S(2)}) collective-permute-start(f32[48,768]{1,0:T(8,128)S(1)} %dynamic-slice_add_fusion.3), channel_id=1, source_target_pairs={{0,8},{4,12},{8,0},{12,4},{16,24},{20,28},{24,16},{28,20},{1,9},{5... | collective-permute-start | bytes 442376 | tf_op jit(solution)/shard_map/ppermute | solution.py:219
  113.7 13.6 %collective-permute-start.9 = (f32[48,768]{1,0:T(8,128)S(1)}, f32[48,768]{1,0:T(8,128)S(1)}, u32[]{:S(2)}, u32[]{:S(2)}) collective-permute-start(f32[48,768]{1,0:T(8,128)S(1)} %add.103), channel_id=1, source_target_pairs={{0,16},{4,20},{8,24},{12,28},{16,0},{20,4},{24,8},{28,12},{1,17},{... | collective-permute-start | bytes 442376 | tf_op jit(solution)/shard_map/ppermute | solution.py:219
  116.5 12.8 %collective-permute-start.15 = (f32[48,768]{1,0:T(8,128)S(1)}, f32[48,768]{1,0:T(8,128)S(1)}, u32[]{:S(2)}, u32[]{:S(2)}) collective-permute-start(f32[48,768]{1,0:T(8,128)S(1)} %add.111), channel_id=1, source_target_pairs={{0,16},{4,20},{8,24},{12,28},{16,0},{20,4},{24,8},{28,12},{1,17},{... | collective-permute-start | bytes 442376 | tf_op jit(solution)/shard_map/ppermute | solution.py:219
  127.4 5.2 %collective-permute-start.10 = (f32[48,768]{1,0:T(8,128)S(1)}, f32[48,768]{1,0:T(8,128)S(1)}, u32[]{:S(2)}, u32[]{:S(2)}) collective-permute-start(f32[48,768]{1,0:T(8,128)S(1)} %add.104), channel_id=1, source_target_pairs={{0,4},{4,0},{8,12},{12,8},{16,20},{20,16},{24,28},{28,24},{1,5},{5... | collective-permute-start | bytes 442376 | tf_op jit(solution)/shard_map/ppermute | solution.py:219
  129.2 6.8 %collective-permute-start.16 = (f32[48,768]{1,0:T(8,128)S(1)}, f32[48,768]{1,0:T(8,128)S(1)}, u32[]{:S(2)}, u32[]{:S(2)}) collective-permute-start(f32[48,768]{1,0:T(8,128)S(1)} %add.112), channel_id=1, source_target_pairs={{0,2},{1,3},{2,0},{3,1},{4,6},{5,7},{6,4},{7,5},{8,10},{9,11},{10,... | collective-permute-start | bytes 442376 | tf_op jit(solution)/shard_map/ppermute | solution.py:219
  132.6 7.6 %collective-permute-start.11 = (f32[96,768]{1,0:T(8,128)S(1)}, f32[96,768]{1,0:T(8,128)S(1)}, u32[]{:S(2)}, u32[]{:S(2)}) collective-permute-start(f32[96,768]{1,0:T(8,128)S(1)} %pad_maximum_fusion.4), channel_id=1, source_target_pairs={{0,2},{1,3},{2,0},{3,1},{4,6},{5,7},{6,4},{7,5},{8,10},{9,11},{10,... | collective-permute-start | bytes 884744 | tf_op jit(solution)/shard_map/ppermute | solution.py:219
  136.1 6.8 %collective-permute-start.17 = (f32[96,768]{1,0:T(8,128)S(1)}, f32[96,768]{1,0:T(8,128)S(1)}, u32[]{:S(2)}, u32[]{:S(2)}) collective-permute-start(f32[96,768]{1,0:T(8,128)S(1)} %pad_maximum_fusion.5), channel_id=1, source_target_pairs={{0,4},{4,0},{8,12},{12,8},{16,20},{20,16},{24,28},{28,24},{1,5},{5... | collective-permute-start | bytes 884744 | tf_op jit(solution)/shard_map/ppermute | solution.py:219
  136.8 7.3 %collective-permute-start.2 = (f32[1,2,192]{2,1,0:T(2,128)S(1)}, f32[1,2,192]{2,1,0:T(2,128)S(1)}, u32[]{:S(2)}, u32[]{:S(2)}) collective-permute-start(f32[1,2,192]{2,1,0:T(2,128)S(1)} %bitcast.23), channel_id=1, source_target_pairs={{0,4},{4,0},{8,12},{12,8},{16,20},{20,16},{24,28},{28,24},{1,5},{5... | collective-permute-start | bytes 4616 | tf_op jit(solution)/shard_map/ppermute | solution.py:219
  144.1 14.7 %collective-permute-start.18 = (f32[384,768]{1,0:T(8,128)}, f32[384,768]{1,0:T(8,128)}, u32[]{:S(2)}, u32[]{:S(2)}) collective-permute-start(f32[384,768]{1,0:T(8,128)} %pad_maximum_fusion.3), channel_id=1, source_target_pairs={{0,1},{1,0},{2,3},{3,2},{4,5},{5,4},{6,7},{7,6},{8,9},{9,8},{10,11... | collective-permute-start | bytes 3538952 | tf_op jit(solution)/shard_map/ppermute | solution.py:219
  144.1 3.7 %collective-permute-start.3 = (f32[2,2,192]{2,1,0:T(2,128)S(1)}, f32[2,2,192]{2,1,0:T(2,128)S(1)}, u32[]{:S(2)}, u32[]{:S(2)}) collective-permute-start(f32[2,2,192]{2,1,0:T(2,128)S(1)} %pad_maximum_fusion.9), channel_id=1, source_target_pairs={{0,8},{4,12},{8,0},{12,4},{16,24},{20,28},{24,16},{28,20},{1,9},{5... | collective-permute-start | bytes 9224 | tf_op jit(solution)/shard_map/ppermute | solution.py:219
  147.8 4.6 %collective-permute-start.4 = (f32[4,2,192]{2,1,0:T(2,128)S(1)}, f32[4,2,192]{2,1,0:T(2,128)S(1)}, u32[]{:S(2)}, u32[]{:S(2)}) collective-permute-start(f32[4,2,192]{2,1,0:T(2,128)S(1)} %pad_maximum_fusion.6), channel_id=1, source_target_pairs={{0,16},{4,20},{8,24},{12,28},{16,0},{20,4},{24,8},{28,12},{1,17},{... | collective-permute-start | bytes 18440 | tf_op jit(solution)/shard_map/ppermute | solution.py:219
  177.8 8.0 %copy-start.4 = (f32[4,512,768]{2,1,0:T(8,128)S(1)}, f32[4,512,768]{2,1,0:T(8,128)}, u32[]{:S(2)}) copy-start(f32[4,512,768]{2,1,0:T(8,128)} %get-tuple-element.23) | copy-start | bytes 18874372
  180.1 5.7 %collective-permute-start.21 = (f32[2,512,768]{2,1,0:T(8,128)S(1)}, f32[2,512,768]{2,1,0:T(8,128)S(1)}, u32[]{:S(2)}, u32[]{:S(2)}) collective-permute-start(f32[2,512,768]{2,1,0:T(8,128)S(1)} %slice.69), channel_id=1, source_target_pairs={{0,1},{1,0},{2,3},{3,2},{4,5},{5,4},{6,7},{7,6},{8,9},{9,8},{10,11... | collective-permute-start | bytes 9437192 | tf_op jit(solution)/shard_map/ppermute | solution.py:219
  186.3 36.6 %collective-permute-start.22 = (f32[512,768]{1,0:T(8,128)S(1)}, f32[512,768]{1,0:T(8,128)}, u32[]{:S(2)}, u32[]{:S(2)}) collective-permute-start(f32[512,768]{1,0:T(8,128)S(1)} %slice_bitcast_fusion), channel_id=1, source_target_pairs={{0,2},{1,3},{2,0},{3,1},{4,6},{5,7},{6,4},{7,5},{8,10},{9,11},{10,... | collective-permute-start | bytes 4718600 | tf_op jit(solution)/shard_map/ppermute | solution.py:219
  187.7 1.2 collective-permute-start.23
  189.0 33.9 %copy-start.3 = (f32[512,768]{1,0:T(8,128)S(1)}, f32[512,768]{1,0:T(8,128)}, u32[]{:S(2)}) copy-start(f32[512,768]{1,0:T(8,128)} %copy-done.2) | copy-start | bytes 4718596
  189.0 33.9 %collective-permute-start.24 = (f32[512]{0:T(512)S(1)}, f32[512]{0:T(512)S(1)}, u32[]{:S(2)}, u32[]{:S(2)}) collective-permute-start(f32[512]{0:T(512)S(1)} %bitcast.25), channel_id=1, source_target_pairs={{0,2},{1,3},{2,0},{3,1},{4,6},{5,7},{6,4},{7,5},{8,10},{9,11},{10,... | collective-permute-start | bytes 6152 | tf_op jit(solution)/shard_map/ppermute | solution.py:219
  222.9 3.0 %copy-start.1 = (f32[768,768]{1,0:T(8,128)S(1)}, f32[768,768]{1,0:T(8,128)}, u32[]{:S(2)}) copy-start(f32[768,768]{1,0:T(8,128)} %param.5) | copy-start | bytes 7077892
  (1 other events, 1.2 us)
Sparse Core Ops, SparseCore 0:
  15.6 88.8 all-gather.1

commit v3 on v2

--- a/solution.py
+++ b/solution.py
@@ -13,7 +13,7 @@
 PRIOR_WEIGHT = 0.25
 EPSILON = 1e-06
 GROUP = 4
-TILE = 512
+TILE = 1024
 VMEM_BYTES = 56 * 1024 * 1024
 
 f32, bf16 = jnp.float32, jnp.bfloat16

time: 234 us -> 229 us (0.979)
  Pallas kernels: 60.4 us -> 56.6 us
  transfers between devices with their start and end apart: 26 -> 26, of which waited for: 16 -> 16; matrix products, arithmetic and copies ran while one was open for 8% -> 8% of each run, Pallas kernels for 19% -> 18%
where the time goes in v3:
time: 229 us
  waiting for transfers between devices  93.6 us (41%)
  Pallas kernels  56.6 us (25%)
  starting transfers between devices  29.3 us (13%)
  other arithmetic  21.3 us (9%)
  between operations  14.3 us (6%)
  local copies, waits for them, and re-layouts  9.32 us (4%)
  matrix products  4.35 us (2%)
    ppermute x25, waiting for transfers between devices, swap(): return lax.ppermute(value, axis, [(i, i ^ bit) for i in range(sizes[axis])])  93.6 us
    ppermute x25, starting transfers between devices, swap(): return lax.ppermute(value, axis, [(i, i ^ bit) for i in range(sizes[axis])])  29.3 us
    pallas_call x1, Pallas kernels, cent_partial(): pl.pallas_call(functools.partial(sums_kernel, scale), grid=(number,), in_...  16.1 us
    pallas_call x1, Pallas kernels, cross_partial(): pl.pallas_call(functools.partial(cross_kernel, tiles), grid=(tiles,), in_...  13.7 us
    pallas_call x1, Pallas kernels, polar_update(): pl.pallas_call(polar_kernel, in_specs=[pl.BlockSpec(memory_space=pltpu.VM...  13.5 us
    pallas_call x1, Pallas kernels, row_stats(): pl.pallas_call(functools.partial(stats_kernel, scale), grid=(tiles,), in_...  13.3 us
    concatenate x1, other arithmetic, body(): blocks = jnp.concatenate([pair, other_pair])  5.63 us
  transfers between devices with their start and end apart: 26, of which 16 were waited for; matrix products, arithmetic and copies ran while one was open for 8% of the time, Pallas kernels for 18%

profile of v3, /device:TPU:0, one launch (start us, length us, event | category | flops | bytes accessed | tf_op | source)
XLA Modules:
  0.0 228.8 jit_solution(13923588896897243987)
XLA Ops:
  7.2 1.6 copy-done
  8.8 4.3 %convolution_reduce-precision_fusion.rot_ref = f32[768,768]{1,0:T(8,128)S(1)} fusion(bf16[768,768]{1,0:T(8,128)(2,1)} %emb_ref.1, f32[768,768]{1,0:T(8,128)S(1)} %copy-done), kind=kOutput, calls=%fused_computation.4 | convolution fusion | flops 5436407808 | bytes 5898240 | tf_op jit(solution)/shard_map/dot_general | solution.py:265
  15.5 13.3 %row_stats.1 = (f32[4096,768]{1,0:T(8,128)}, f32[4,1,768]{2,1,0:T(1,128)}, f32[2,768]{1,0:T(2,128)}) custom-call(f32[768,768]{1,0:T(8,128)} %copy-done.5, bf16[4096,768]{1,0:T(8,128)(2,1)} %cent_ref.3), custom_call_target="tpu_custom_call" | custom-call | flops 4831838208 | bytes 18874368 | tf_op jit(solution)/shard_map/row_stats/pallas_call | solution.py:58
  31.1 2.9 %collective-permute-start.1 = (f32[2,768]{1,0:T(2,128)S(1)}, f32[2,768]{1,0:T(2,128)S(1)}, u32[]{:S(2)}, u32[]{:S(2)}) collective-permute-start(f32[2,768]{1,0:T(2,128)S(1)} %pad_maximum_fusion.8), channel_id=1, source_target_pairs={{0,2},{1,3},{2,0},{3,1},{4,6},{5,7},{6,4},{7,5},{8,10},{9,11},{10,... | collective-permute-start | bytes 18440 | tf_op jit(solution)/shard_map/ppermute | solution.py:219
  34.1 1.6 collective-permute-done.1
  36.3 13.7 %cross_partial.1 = f32[768,768]{1,0:T(8,128)} custom-call(f32[4096,768]{1,0:T(8,128)} %get-tuple-element.16.exp_ref, f32[4,1,768]{2,1,0:T(1,128)} %get-tuple-element.17.tile_top_ref, f32[2,768]{1,0:T(2,128)} %pad_maximum_fusion.7.stat_ref, bf16[4096,768]{1,0:T(8,128)(2,1)} %cent_ref.3, bf16[768,768]{1,0:T(8,128)(2,1)} %emb_ref.1), custom_call_target="tpu_custom_call" | custom-call | flops 4831838208 | bytes 18874368 | tf_op jit(solution)/shard_map/cross_partial/pallas_call | solution.py:111
  52.7 2.1 collective-permute-start.19
  54.8 1.8 dynamic-slice_add_fusion
  56.7 1.7 collective-permute-start.6
  58.5 1.6 collective-permute-start.12
  60.1 36.1 %collective-permute-done.6 = f32[96,768]{1,0:T(8,128)S(1)} collective-permute-done((f32[96,768]{1,0:T(8,128)S(1)}, f32[96,768]{1,0:T(8,128)S(1)}, u32[]{:S(2)}, u32[]{:S(2)}) %collective-permute-start.6) | collective-permute-done | bytes 294944 | tf_op jit(solution)/shard_map/ppermute | solution.py:219
  96.2 1.8 collective-permute-start.7
  99.7 3.3 %pad_maximum_fusion.1 = f32[2,512,768]{2,1,0:T(8,128)} fusion(f32[1,512,768]{2,1,0:T(8,128)} %bitcast.3, f32[1,512,768]{2,1,0:T(8,128)S(1)} %bitcast.21), kind=kLoop, calls=%fused_computation.1 | loop fusion | flops 786432 | bytes 6291456 | tf_op jit(solution)/shard_map/stack | solution.py:288
  103.0 1.6 collective-permute-start.8
  105.2 4.5 %collective-permute-done.8 = f32[48,768]{1,0:T(8,128)S(1)} collective-permute-done((f32[48,768]{1,0:T(8,128)S(1)}, f32[48,768]{1,0:T(8,128)S(1)}, u32[]{:S(2)}, u32[]{:S(2)}) %collective-permute-start.8) | collective-permute-done | bytes 147488 | tf_op jit(solution)/shard_map/ppermute | solution.py:219
  109.7 2.6 %collective-permute-start.9 = (f32[48,768]{1,0:T(8,128)S(1)}, f32[48,768]{1,0:T(8,128)S(1)}, u32[]{:S(2)}, u32[]{:S(2)}) collective-permute-start(f32[48,768]{1,0:T(8,128)S(1)} %add.103), channel_id=1, source_target_pairs={{0,16},{4,20},{8,24},{12,28},{16,0},{20,4},{24,8},{28,12},{1,17},{... | collective-permute-start | bytes 442376 | tf_op jit(solution)/shard_map/ppermute | solution.py:219
  112.5 3.0 %collective-permute-start.15 = (f32[48,768]{1,0:T(8,128)S(1)}, f32[48,768]{1,0:T(8,128)S(1)}, u32[]{:S(2)}, u32[]{:S(2)}) collective-permute-start(f32[48,768]{1,0:T(8,128)S(1)} %add.111), channel_id=1, source_target_pairs={{0,16},{4,20},{8,24},{12,28},{16,0},{20,4},{24,8},{28,12},{1,17},{... | collective-permute-start | bytes 442376 | tf_op jit(solution)/shard_map/ppermute | solution.py:219
  115.5 7.7 %collective-permute-done.9 = f32[48,768]{1,0:T(8,128)S(1)} collective-permute-done((f32[48,768]{1,0:T(8,128)S(1)}, f32[48,768]{1,0:T(8,128)S(1)}, u32[]{:S(2)}, u32[]{:S(2)}) %collective-permute-start.9) | collective-permute-done | bytes 147488 | tf_op jit(solution)/shard_map/ppermute | solution.py:219
  125.9 2.6 %collective-permute-done.10 = f32[48,768]{1,0:T(8,128)S(1)} collective-permute-done((f32[48,768]{1,0:T(8,128)S(1)}, f32[48,768]{1,0:T(8,128)S(1)}, u32[]{:S(2)}, u32[]{:S(2)}) %collective-permute-start.10) | collective-permute-done | bytes 147488 | tf_op jit(solution)/shard_map/ppermute | solution.py:219
  129.1 3.0 %collective-permute-done.16 = f32[48,768]{1,0:T(8,128)S(1)} collective-permute-done((f32[48,768]{1,0:T(8,128)S(1)}, f32[48,768]{1,0:T(8,128)S(1)}, u32[]{:S(2)}, u32[]{:S(2)}) %collective-permute-start.16) | collective-permute-done | bytes 147488 | tf_op jit(solution)/shard_map/ppermute | solution.py:219
  134.4 2.0 collective-permute-done.11
  136.5 2.5 %collective-permute-done.17 = f32[96,768]{1,0:T(8,128)S(1)} collective-permute-done((f32[96,768]{1,0:T(8,128)S(1)}, f32[96,768]{1,0:T(8,128)S(1)}, u32[]{:S(2)}, u32[]{:S(2)}) %collective-permute-start.17) | collective-permute-done | bytes 294944 | tf_op jit(solution)/shard_map/ppermute | solution.py:219
  141.2 2.6 %collective-permute-done.3 = f32[2,2,192]{2,1,0:T(2,128)S(1)} collective-permute-done((f32[2,2,192]{2,1,0:T(2,128)S(1)}, f32[2,2,192]{2,1,0:T(2,128)S(1)}, u32[]{:S(2)}, u32[]{:S(2)}) %collective-permute-start.3) | collective-permute-done | bytes 3104 | tf_op jit(solution)/shard_map/ppermute | solution.py:219
  143.8 2.4 %collective-permute-start.4 = (f32[4,2,192]{2,1,0:T(2,128)S(1)}, f32[4,2,192]{2,1,0:T(2,128)S(1)}, u32[]{:S(2)}, u32[]{:S(2)}) collective-permute-start(f32[4,2,192]{2,1,0:T(2,128)S(1)} %pad_maximum_fusion.6), channel_id=1, source_target_pairs={{0,16},{4,20},{8,24},{12,28},{16,0},{20,4},{24,8},{28,12},{1,17},{... | collective-permute-start | bytes 18440 | tf_op jit(solution)/shard_map/ppermute | solution.py:219
  146.3 2.2 collective-permute-done.4
  149.2 5.6 %pad_maximum_fusion.cent_ref = f32[4,512,768]{2,1,0:T(8,128)} fusion(f32[2,512,768]{2,1,0:T(8,128)} %collective-permute-done.20, f32[1,512,768]{2,1,0:T(8,128)} %bitcast.3, f32[1,512,768]{2,1,0:T(8,128)S(1)} %bitcast.22), kind=kLoop, calls=%fused_computation | loop fusion | flops 3145728 | bytes 12582912 | tf_op jit(solution)/shard_map/concatenate | solution.py:290
  157.8 16.1 %cent_partial.1 = (f32[4,512,768]{2,1,0:T(8,128)}, f32[4,512,128]{2,1,0:T(8,128)}) custom-call(f32[1536,768]{1,0:T(8,128)} %all-gather.2.cloned.1.call-done.rows_ref, f32[2,1536]{1,0:T(2,128)} %reshape.10.stat_ref, f32[4,512,768]{2,1,0:T(8,128)} %pad_maximum_fusion.cent_ref), custom_call_target="tpu_custom_call" | custom-call | flops 9663676416 | bytes 17301504 | tf_op jit(solution)/shard_map/cent_partial/pallas_call | solution.py:149
  173.9 2.2 slice.69
  176.2 5.6 %collective-permute-done.21 = f32[2,512,768]{2,1,0:T(8,128)S(1)} collective-permute-done((f32[2,512,768]{2,1,0:T(8,128)S(1)}, f32[2,512,768]{2,1,0:T(8,128)S(1)}, u32[]{:S(2)}, u32[]{:S(2)}) %collective-permute-start.21) | collective-permute-done | bytes 3145760 | tf_op jit(solution)/shard_map/ppermute | solution.py:219
  186.1 13.5 %polar_update.1 = f32[768,768]{1,0:T(8,128)} custom-call(f32[768,768]{1,0:T(8,128)} %pad_maximum_fusion.2.cross_ref), custom_call_target="tpu_custom_call" | custom-call | flops 8153726976 | bytes 4718592 | tf_op jit(solution)/shard_map/polar_update/pallas_call | solution.py:198
  199.6 19.4 %collective-permute-done.24 = f32[512]{0:T(512)S(1)} collective-permute-done((f32[512]{0:T(512)S(1)}, f32[512]{0:T(512)S(1)}, u32[]{:S(2)}, u32[]{:S(2)}) %collective-permute-start.24) | collective-permute-done | bytes 2080 | tf_op jit(solution)/shard_map/ppermute | solution.py:219
  219.0 2.9 %fusion.2 = f32[512,768]{1,0:T(8,128)} fusion(f32[512,768]{1,0:T(8,128)} %collective-permute-done.22, f32[2,512,768]{2,1,0:T(8,128)S(1)} %slice_add_fusion, f32[512,768]{1,0:T(8,128)S(1)} %copy-done.3, f32[512]{0:T(512)S(1)} %add_add_fusion), kind=kLoop, calls=%fused_computation.9 | loop fusion | flops 1572864 | bytes 6293504 | tf_op jit(solution)/shard_map/div | solution.py:302
  (89 shorter events, 26.2 us)
Async XLA Ops:
  7.2 1.7 copy-start
  7.2 116.1 %all-gather.2.cloned.1.call-start = ((), (), s32[]{:S(2)}) async-start(), calls=%async_computation | async-start | bytes 5308416 | tf_op jit(solution)/shard_map/all_gather | solution.py:270
  13.2 1.4 copy-start.5
  28.8 1.5 collective-permute-start
  31.1 4.5 %collective-permute-start.1 = (f32[2,768]{1,0:T(2,128)S(1)}, f32[2,768]{1,0:T(2,128)S(1)}, u32[]{:S(2)}, u32[]{:S(2)}) collective-permute-start(f32[2,768]{1,0:T(2,128)S(1)} %pad_maximum_fusion.8), channel_id=1, source_target_pairs={{0,2},{1,3},{2,0},{3,1},{4,6},{5,7},{6,4},{7,5},{8,10},{9,11},{10,... | collective-permute-start | bytes 18440 | tf_op jit(solution)/shard_map/ppermute | solution.py:219
  51.3 3.4 %collective-permute-start.5 = (f32[384,768]{1,0:T(8,128)S(1)}, f32[384,768]{1,0:T(8,128)}, u32[]{:S(2)}, u32[]{:S(2)}) collective-permute-start(f32[384,768]{1,0:T(8,128)S(1)} %constant_dynamic-slice_fusion.4), channel_id=1, source_target_pairs={{0,1},{1,0},{2,3},{3,2},{4,5},{5,4},{6,7},{7,6},{8,9},{9,8},{10,11... | collective-permute-start | bytes 3538952 | tf_op jit(solution)/shard_map/ppermute | solution.py:219
  52.7 96.5 %copy-start.2 = (f32[512,768]{1,0:T(8,128)}, f32[512,768]{1,0:T(8,128)S(1)}, u32[]{:S(2)}) copy-start(f32[512,768]{1,0:T(8,128)S(1)} %dynamic-slice_convert_fusion) | copy-start | bytes 4718596
  52.7 47.0 %collective-permute-start.19 = (f32[512,768]{1,0:T(8,128)S(1)}, f32[512,768]{1,0:T(8,128)}, u32[]{:S(2)}, u32[]{:S(2)}) collective-permute-start(f32[512,768]{1,0:T(8,128)S(1)} %dynamic-slice_convert_fusion), channel_id=1, source_target_pairs={{0,2},{1,3},{2,0},{3,1},{4,6},{5,7},{6,4},{7,5},{8,10},{9,11},{10,... | collective-permute-start | bytes 4718600 | tf_op jit(solution)/shard_map/ppermute | solution.py:219
  56.7 39.4 %collective-permute-start.6 = (f32[96,768]{1,0:T(8,128)S(1)}, f32[96,768]{1,0:T(8,128)S(1)}, u32[]{:S(2)}, u32[]{:S(2)}) collective-permute-start(f32[96,768]{1,0:T(8,128)S(1)} %constant_dynamic-slice_fusion.3), channel_id=1, source_target_pairs={{0,2},{1,3},{2,0},{3,1},{4,6},{5,7},{6,4},{7,5},{8,10},{9,11},{10,... | collective-permute-start | bytes 884744 | tf_op jit(solution)/shard_map/ppermute | solution.py:219
  58.5 39.5 %collective-permute-start.12 = (f32[96,768]{1,0:T(8,128)S(1)}, f32[96,768]{1,0:T(8,128)S(1)}, u32[]{:S(2)}, u32[]{:S(2)}) collective-permute-start(f32[96,768]{1,0:T(8,128)S(1)} %constant_dynamic-slice_fusion.1), channel_id=1, source_target_pairs={{0,4},{4,0},{8,12},{12,8},{16,20},{20,16},{24,28},{28,24},{1,5},{5... | collective-permute-start | bytes 884744 | tf_op jit(solution)/shard_map/ppermute | solution.py:219
  96.2 6.8 %collective-permute-start.7 = (f32[48,768]{1,0:T(8,128)S(1)}, f32[48,768]{1,0:T(8,128)S(1)}, u32[]{:S(2)}, u32[]{:S(2)}) collective-permute-start(f32[48,768]{1,0:T(8,128)S(1)} %constant_dynamic-slice_fusion.2), channel_id=1, source_target_pairs={{0,4},{4,0},{8,12},{12,8},{16,20},{20,16},{24,28},{28,24},{1,5},{5... | collective-permute-start | bytes 442376 | tf_op jit(solution)/shard_map/ppermute | solution.py:219
  98.1 6.6 %collective-permute-start.13 = (f32[48,768]{1,0:T(8,128)S(1)}, f32[48,768]{1,0:T(8,128)S(1)}, u32[]{:S(2)}, u32[]{:S(2)}) collective-permute-start(f32[48,768]{1,0:T(8,128)S(1)} %constant_dynamic-slice_fusion), channel_id=1, source_target_pairs={{0,2},{1,3},{2,0},{3,1},{4,6},{5,7},{6,4},{7,5},{8,10},{9,11},{10,... | collective-permute-start | bytes 442376 | tf_op jit(solution)/shard_map/ppermute | solution.py:219
  103.0 46.2 %collective-permute-start.20 = (f32[2,512,768]{2,1,0:T(8,128)}, f32[2,512,768]{2,1,0:T(8,128)}, u32[]{:S(2)}, u32[]{:S(2)}) collective-permute-start(f32[2,512,768]{2,1,0:T(8,128)} %pad_maximum_fusion.1), channel_id=1, source_target_pairs={{0,1},{1,0},{2,3},{3,2},{4,5},{5,4},{6,7},{7,6},{8,9},{9,8},{10,11... | collective-permute-start | bytes 9437192 | tf_op jit(solution)/shard_map/ppermute | solution.py:219
  103.0 6.7 %collective-permute-start.8 = (f32[48,768]{1,0:T(8,128)S(1)}, f32[48,768]{1,0:T(8,128)S(1)}, u32[]{:S(2)}, u32[]{:S(2)}) collective-permute-start(f32[48,768]{1,0:T(8,128)S(1)} %dynamic-slice_add_fusion.4), channel_id=1, source_target_pairs={{0,8},{4,12},{8,0},{12,4},{16,24},{20,28},{24,16},{28,20},{1,9},{5... | collective-permute-start | bytes 442376 | tf_op jit(solution)/shard_map/ppermute | solution.py:219
  104.7 7.8 %collective-permute-start.14 = (f32[48,768]{1,0:T(8,128)S(1)}, f32[48,768]{1,0:T(8,128)S(1)}, u32[]{:S(2)}, u32[]{:S(2)}) collective-permute-start(f32[48,768]{1,0:T(8,128)S(1)} %dynamic-slice_add_fusion.3), channel_id=1, source_target_pairs={{0,8},{4,12},{8,0},{12,4},{16,24},{20,28},{24,16},{28,20},{1,9},{5... | collective-permute-start | bytes 442376 | tf_op jit(solution)/shard_map/ppermute | solution.py:219
  109.7 13.5 %collective-permute-start.9 = (f32[48,768]{1,0:T(8,128)S(1)}, f32[48,768]{1,0:T(8,128)S(1)}, u32[]{:S(2)}, u32[]{:S(2)}) collective-permute-start(f32[48,768]{1,0:T(8,128)S(1)} %add.103), channel_id=1, source_target_pairs={{0,16},{4,20},{8,24},{12,28},{16,0},{20,4},{24,8},{28,12},{1,17},{... | collective-permute-start | bytes 442376 | tf_op jit(solution)/shard_map/ppermute | solution.py:219
  112.5 12.8 %collective-permute-start.15 = (f32[48,768]{1,0:T(8,128)S(1)}, f32[48,768]{1,0:T(8,128)S(1)}, u32[]{:S(2)}, u32[]{:S(2)}) collective-permute-start(f32[48,768]{1,0:T(8,128)S(1)} %add.111), channel_id=1, source_target_pairs={{0,16},{4,20},{8,24},{12,28},{16,0},{20,4},{24,8},{28,12},{1,17},{... | collective-permute-start | bytes 442376 | tf_op jit(solution)/shard_map/ppermute | solution.py:219
  123.3 5.2 %collective-permute-start.10 = (f32[48,768]{1,0:T(8,128)S(1)}, f32[48,768]{1,0:T(8,128)S(1)}, u32[]{:S(2)}, u32[]{:S(2)}) collective-permute-start(f32[48,768]{1,0:T(8,128)S(1)} %add.104), channel_id=1, source_target_pairs={{0,4},{4,0},{8,12},{12,8},{16,20},{20,16},{24,28},{28,24},{1,5},{5... | collective-permute-start | bytes 442376 | tf_op jit(solution)/shard_map/ppermute | solution.py:219
  125.3 6.8 %collective-permute-start.16 = (f32[48,768]{1,0:T(8,128)S(1)}, f32[48,768]{1,0:T(8,128)S(1)}, u32[]{:S(2)}, u32[]{:S(2)}) collective-permute-start(f32[48,768]{1,0:T(8,128)S(1)} %add.112), channel_id=1, source_target_pairs={{0,2},{1,3},{2,0},{3,1},{4,6},{5,7},{6,4},{7,5},{8,10},{9,11},{10,... | collective-permute-start | bytes 442376 | tf_op jit(solution)/shard_map/ppermute | solution.py:219
  128.6 7.9 %collective-permute-start.11 = (f32[96,768]{1,0:T(8,128)S(1)}, f32[96,768]{1,0:T(8,128)S(1)}, u32[]{:S(2)}, u32[]{:S(2)}) collective-permute-start(f32[96,768]{1,0:T(8,128)S(1)} %pad_maximum_fusion.4), channel_id=1, source_target_pairs={{0,2},{1,3},{2,0},{3,1},{4,6},{5,7},{6,4},{7,5},{8,10},{9,11},{10,... | collective-permute-start | bytes 884744 | tf_op jit(solution)/shard_map/ppermute | solution.py:219
  132.2 6.8 %collective-permute-start.17 = (f32[96,768]{1,0:T(8,128)S(1)}, f32[96,768]{1,0:T(8,128)S(1)}, u32[]{:S(2)}, u32[]{:S(2)}) collective-permute-start(f32[96,768]{1,0:T(8,128)S(1)} %pad_maximum_fusion.5), channel_id=1, source_target_pairs={{0,4},{4,0},{8,12},{12,8},{16,20},{20,16},{24,28},{28,24},{1,5},{5... | collective-permute-start | bytes 884744 | tf_op jit(solution)/shard_map/ppermute | solution.py:219
  132.8 7.3 %collective-permute-start.2 = (f32[1,2,192]{2,1,0:T(2,128)S(1)}, f32[1,2,192]{2,1,0:T(2,128)S(1)}, u32[]{:S(2)}, u32[]{:S(2)}) collective-permute-start(f32[1,2,192]{2,1,0:T(2,128)S(1)} %bitcast.23), channel_id=1, source_target_pairs={{0,4},{4,0},{8,12},{12,8},{16,20},{20,16},{24,28},{28,24},{1,5},{5... | collective-permute-start | bytes 4616 | tf_op jit(solution)/shard_map/ppermute | solution.py:219
  140.1 14.7 %collective-permute-start.18 = (f32[384,768]{1,0:T(8,128)}, f32[384,768]{1,0:T(8,128)}, u32[]{:S(2)}, u32[]{:S(2)}) collective-permute-start(f32[384,768]{1,0:T(8,128)} %pad_maximum_fusion.3), channel_id=1, source_target_pairs={{0,1},{1,0},{2,3},{3,2},{4,5},{5,4},{6,7},{7,6},{8,9},{9,8},{10,11... | collective-permute-start | bytes 3538952 | tf_op jit(solution)/shard_map/ppermute | solution.py:219
  140.2 3.7 %collective-permute-start.3 = (f32[2,2,192]{2,1,0:T(2,128)S(1)}, f32[2,2,192]{2,1,0:T(2,128)S(1)}, u32[]{:S(2)}, u32[]{:S(2)}) collective-permute-start(f32[2,2,192]{2,1,0:T(2,128)S(1)} %pad_maximum_fusion.9), channel_id=1, source_target_pairs={{0,8},{4,12},{8,0},{12,4},{16,24},{20,28},{24,16},{28,20},{1,9},{5... | collective-permute-start | bytes 9224 | tf_op jit(solution)/shard_map/ppermute | solution.py:219
  143.8 4.6 %collective-permute-start.4 = (f32[4,2,192]{2,1,0:T(2,128)S(1)}, f32[4,2,192]{2,1,0:T(2,128)S(1)}, u32[]{:S(2)}, u32[]{:S(2)}) collective-permute-start(f32[4,2,192]{2,1,0:T(2,128)S(1)} %pad_maximum_fusion.6), channel_id=1, source_target_pairs={{0,16},{4,20},{8,24},{12,28},{16,0},{20,4},{24,8},{28,12},{1,17},{... | collective-permute-start | bytes 18440 | tf_op jit(solution)/shard_map/ppermute | solution.py:219
  173.9 8.0 %copy-start.4 = (f32[4,512,768]{2,1,0:T(8,128)S(1)}, f32[4,512,768]{2,1,0:T(8,128)}, u32[]{:S(2)}) copy-start(f32[4,512,768]{2,1,0:T(8,128)} %get-tuple-element.23) | copy-start | bytes 18874372
  176.1 5.7 %collective-permute-start.21 = (f32[2,512,768]{2,1,0:T(8,128)S(1)}, f32[2,512,768]{2,1,0:T(8,128)S(1)}, u32[]{:S(2)}, u32[]{:S(2)}) collective-permute-start(f32[2,512,768]{2,1,0:T(8,128)S(1)} %slice.69), channel_id=1, source_target_pairs={{0,1},{1,0},{2,3},{3,2},{4,5},{5,4},{6,7},{7,6},{8,9},{9,8},{10,11... | collective-permute-start | bytes 9437192 | tf_op jit(solution)/shard_map/ppermute | solution.py:219
  182.3 36.6 %collective-permute-start.22 = (f32[512,768]{1,0:T(8,128)S(1)}, f32[512,768]{1,0:T(8,128)}, u32[]{:S(2)}, u32[]{:S(2)}) collective-permute-start(f32[512,768]{1,0:T(8,128)S(1)} %slice_bitcast_fusion), channel_id=1, source_target_pairs={{0,2},{1,3},{2,0},{3,1},{4,6},{5,7},{6,4},{7,5},{8,10},{9,11},{10,... | collective-permute-start | bytes 4718600 | tf_op jit(solution)/shard_map/ppermute | solution.py:219
  183.8 1.2 collective-permute-start.23
  185.0 33.9 %copy-start.3 = (f32[512,768]{1,0:T(8,128)S(1)}, f32[512,768]{1,0:T(8,128)}, u32[]{:S(2)}) copy-start(f32[512,768]{1,0:T(8,128)} %copy-done.2) | copy-start | bytes 4718596
  185.1 33.9 %collective-permute-start.24 = (f32[512]{0:T(512)S(1)}, f32[512]{0:T(512)S(1)}, u32[]{:S(2)}, u32[]{:S(2)}) collective-permute-start(f32[512]{0:T(512)S(1)} %bitcast.25), channel_id=1, source_target_pairs={{0,2},{1,3},{2,0},{3,1},{4,6},{5,7},{6,4},{7,5},{8,10},{9,11},{10,... | collective-permute-start | bytes 6152 | tf_op jit(solution)/shard_map/ppermute | solution.py:219
  219.0 3.0 %copy-start.1 = (f32[768,768]{1,0:T(8,128)S(1)}, f32[768,768]{1,0:T(8,128)}, u32[]{:S(2)}) copy-start(f32[768,768]{1,0:T(8,128)} %param.5) | copy-start | bytes 7077892
  (1 other events, 1.2 us)
Sparse Core Ops, SparseCore 0:
  15.6 88.8 all-gather.1
